TPU v7x, 128 devices: a whole 4x4x4 slice. The times are simulated.
128 devices in a mesh: slab: 8 (over x, core), patch: 16 (over z, y).
Axes of the slice: x: 4, y: 4, z: 4, core: 2. Of those that a mesh axis runs over, the one named last changes fastest.
Arguments:
- coarse: bfloat16 [12, 1024, 4096], P(None, 'slab', 'patch'), may hold values from -6 to 6
- latent: float32 [12, 1024, 4096], P(None, 'slab', 'patch'), may hold values from -6 to 6
- noise_level: float32 [1], replicated, may hold values from 0.3 to 3
- reg_first: bfloat16 [9, 128, 12], replicated, may hold values from -0.625 to 0.625
- reg_second: bfloat16 [9, 12, 128], replicated, may hold values from -0.1875 to 0.1875
- den_first: bfloat16 [9, 128, 24], replicated, may hold values from -0.4375 to 0.4375
- den_middle: bfloat16 [128, 128], replicated, may hold values from -0.5 to 0.5
- den_pool: bfloat16 [128, 128], replicated, may hold values from -2 to 2
- den_last: bfloat16 [9, 12, 128], replicated, may hold values from -0.1875 to 0.1875
- anchors: int32 [8, 16, 2], P('slab'), may hold values from 0 to 3872, as said below
- patch_count: int32 [8], P('slab'), may hold values from 1 to 16, 96 in all
- patch_weight: int32 [224, 224], replicated, may hold values from 1 to 4
Outputs:
- next_state: float32 [12, 1024, 4096], P(None, 'slab', 'patch')
- estimate: float32 [12, 1024, 4096], P(None, 'slab', 'patch')
Inputs may be any that keep to these rules, and one draw needn't show every extreme that they name: anchors[s, k] is the top row and left column of patch k of slab s; the row lies between s * 128 - 224 // 2 and s * 128 + 128 - 224 // 2, within 0 to 800; the column lies within 0 to 3872; patch 0 of every slab stands at column 0 and patch 1 at column 3872. Slab s denoises the entries 0 to patch_count[s] - 1 of its table.
All inputs are finite; a program needn't handle non-finite values. No bound on the sum of `patch_count` on one device may be relied on, other than what follows from the above.
Results may differ from a plain program's by a relative error of at most 0.0028.
Values may be sent and summed in bfloat16 or wider, within the bound.
A program may use at most 192 MiB of HBM per device.

v0:
```python
import jax
import jax.numpy as jnp
from jax import lax
from jax.sharding import PartitionSpec as P

sigma_data = 0.5
step_ratio = 0.6


def with_halo(cells, sides, width):
    for axis, dim in sides:
        count = lax.axis_size(axis)
        ends = count - 1
        head = lax.slice_in_dim(cells, 0, width, axis=dim)
        tail = lax.slice_in_dim(cells, cells.shape[dim] - width, cells.shape[dim], axis=dim)
        cells = jnp.concatenate(
            [
                lax.ppermute(tail, axis, [(i, (i + 1) % count) for i in range(ends)]),
                cells,
                lax.ppermute(head, axis, [((i + 1) % count, i) for i in range(ends)]),
            ],
            axis=dim,
        )
    return cells


def passed_along(block, axis, distance):
    devices = range(lax.axis_size(axis))
    route = [(i - distance, i) for i in devices if i - distance in devices]
    return lax.ppermute(block, axis, route)


def conv_gather(padded, weight, height, breadth):
    channels = padded.shape[0]
    outputs = weight.shape[1]
    stacked = jnp.concatenate(
        [
            padded[:, shift_r : shift_r + height, shift_c : shift_c + breadth]
            for shift_r in range(3)
            for shift_c in range(3)
        ],
        0,
    )
    stacked = stacked.reshape(9 * channels, height * breadth)
    flat_weight = jnp.transpose(weight, (1, 0, 2)).reshape(outputs, 9 * channels)
    return jnp.dot(flat_weight, stacked, preferred_element_type=jnp.float32).reshape(
        outputs, height, breadth
    )


def conv_spread(padded, weight, height, breadth):
    channels, full_rows, full_cols = padded.shape
    outputs = weight.shape[1]
    flat = jnp.dot(
        weight.reshape(9 * outputs, channels),
        padded.reshape(channels, full_rows * full_cols),
        preferred_element_type=jnp.float32,
    )
    flat = flat.reshape(9, outputs, full_rows, full_cols)
    total = None
    for shift_r in range(3):
        for shift_c in range(3):
            term = flat[
                3 * shift_r + shift_c, :, shift_r : shift_r + height, shift_c : shift_c + breadth
            ]
            total = term if total is None else total + term
    return total


def pad_one(field):
    return jnp.pad(field, ((0, 0), (1, 1), (1, 1)))


def mix_inner(first, middle, pool, pooled):
    width, height, breadth = first.shape
    lift = jnp.dot(pool.astype(jnp.float32), pooled, precision=lax.Precision.HIGHEST)
    inner = jnp.dot(
        middle, first.reshape(width, height * breadth), preferred_element_type=jnp.float32
    )
    return jax.nn.silu(inner + lift[:, None]).astype(jnp.bfloat16).reshape(width, height, breadth)


def denoise(piece, first, middle, pool, last):
    size = piece.shape[1]
    hidden = jax.nn.silu(conv_gather(pad_one(piece), first, size, size)).astype(jnp.bfloat16)
    pooled = jnp.sum(hidden.astype(jnp.float32), axis=(1, 2)) / (size * size)
    inner = mix_inner(hidden, middle, pool, pooled)
    return conv_spread(pad_one(inner), last, size, size)


def precondition(noise_level):
    level = noise_level[0]
    spread = level * level + sigma_data * sigma_data
    return (
        1.0 / jnp.sqrt(spread),
        sigma_data * sigma_data / spread,
        level * sigma_data / jnp.sqrt(spread),
    )


def add_patch(totals, source, row, column, weight, models):
    size = weight.shape[0]
    start = (jnp.int32(0), row, column)
    piece = lax.dynamic_slice(source, start, (source.shape[0], size, size))
    output = denoise(piece, models[0], models[1], models[2], models[3])
    term = jnp.concatenate([output * weight, weight[None]], 0)
    old = lax.dynamic_slice(totals, start, term.shape)
    return lax.dynamic_update_slice(totals, old + term, start)


def body(
    coarse,
    latent,
    noise_level,
    reg_first,
    reg_second,
    den_first,
    den_middle,
    den_pool,
    den_last,
    anchors,
    patch_count,
    patch_weight,
):
    channels, height, breadth = latent.shape
    patch = patch_weight.shape[0]
    half = patch // 2
    slab_index = lax.axis_index("slab")
    column_index = lax.axis_index("patch")
    row_start = slab_index * height
    col_start = column_index * breadth
    padded = with_halo(coarse, (("slab", 1), ("patch", 2)), 1)
    hidden = jax.nn.silu(conv_gather(padded, reg_first, height, breadth)).astype(jnp.bfloat16)
    padded = with_halo(hidden, (("slab", 1), ("patch", 2)), 1)
    mean = conv_spread(padded, reg_second, height, breadth)
    scale_in, skip, scale_out = precondition(noise_level)
    condition = jnp.concatenate(
        [(scale_in * latent).astype(jnp.bfloat16), mean.astype(jnp.bfloat16)], 0
    )
    table = anchors[0]
    count = patch_count[0]
    per_slab = table.shape[0]
    weight = patch_weight.astype(jnp.float32)
    models = (den_first, den_middle, den_pool, den_last)
    labels = jnp.arange(per_slab, dtype=jnp.int32)
    rows_band = with_halo(condition, (("slab", 1),), half)
    right_side = passed_along(rows_band[:, :, :patch], "patch", -1)
    framed = jnp.concatenate([rows_band, right_side], 2)
    owned = (labels < count) & (table[:, 1] // breadth == column_index)
    order = jnp.argsort(jnp.where(owned, labels, labels + per_slab))
    number = jnp.sum(owned.astype(jnp.int32))
    row_base = row_start - half

    def visit_own(step, totals):
        slot = order[step]
        return add_patch(
            totals, framed, table[slot, 0] - row_base, table[slot, 1] - col_start, weight, models
        )

    start_totals = jnp.zeros((channels + 1, height + patch, breadth + patch), jnp.float32)
    totals = lax.fori_loop(0, number, visit_own, start_totals)
    incoming = passed_along(totals[:, :, breadth:].astype(jnp.bfloat16), "patch", 1).astype(
        jnp.float32
    )
    totals = totals[:, :, :breadth]
    totals = totals.at[:, :, :patch].add(incoming)
    rims = jnp.concatenate([totals[:, :half], totals[:, height + half :]], 1)
    beside = with_halo(rims.astype(jnp.bfloat16), (("slab", 1),), half).astype(rims.dtype)
    totals = totals[:, half : height + half]
    totals = totals.at[:, :half].add(beside[:, :half])
    totals = totals.at[:, height - half :].add(beside[:, 3 * half :])
    blended = totals[:channels] / (1.0 + totals[channels])
    denoised = skip * latent + scale_out * blended
    next_state = latent + (step_ratio - 1.0) * (latent - denoised)
    return (next_state, mean + denoised)


def solution(mesh):
    return jax.shard_map(
        body,
        mesh=mesh,
        in_specs=(
            P(None, "slab", "patch"),
            P(None, "slab", "patch"),
            P(),
            P(),
            P(),
            P(),
            P(),
            P(),
            P(),
            P("slab", None, None),
            P("slab"),
            P(),
        ),
        out_specs=(P(None, "slab", "patch"), P(None, "slab", "patch")),
        check_vma=False,
    )
```

profile of v0, /device:TPU:99, one launch (start us, length us, event | category | flops | bytes accessed | tf_op | source)
XLA Modules:
  0.0 1092.4 jit_solution(8296929856676636668)
XLA Ops:
  1.6 3.7 collective-permute-start
  5.3 1.9 collective-permute-start.1
  7.2 3.1 collective-permute-done.1
  11.9 4.5 collective-permute-start.3
  16.4 1.9 collective-permute-start.2
  18.3 6.9 collective-permute-done.3
  25.2 6.2 collective-permute-done.2
  35.8 3.9 pad.84
  39.7 8.0 copy.41
  47.7 2.6 fusion.23
  50.3 4.5 multiply_convert_fusion.2
  54.8 3.8 collective-permute-start.4
  58.7 1.9 collective-permute-start.5
  61.4 2.9 collective-permute-done.5
  64.4 1.9 collective-permute-start.6
  66.3 5.5 collective-permute-start.7
  73.1 11.8 %pad_maximum_fusion = bf16[128,130,258]{0,2,1:T(8,128)(2,1)} fusion(bf16[128,130,1]{0,2,1:T(2,128)(2,1)S(1)} %collective-permute-done.7, bf16[128,1,256]{0,2,1:T(8,128)(2,1)S(1)} %collective-permute-done.5, bf16[128,128,256]{0,2,1:T(8,128)(2,1)} %copy-done, bf16[128,1,256]{0,2,1:T(8,128)(2,1)S(1)} %collective-permute-done.4, ...), kind=kLoop, calls=%fused_computation.37 | loop fusion | flops 42931200 | bytes 17172480 | tf_op jit(solution)/shard_map/concatenate | solution.py:16
  84.9 13.1 %reshape.173 = bf16[128,33540]{0,1:T(8,128)(2,1)} reshape(bf16[128,130,258]{0,2,1:T(8,128)(2,1)} %pad_maximum_fusion) | data formatting | bytes 17172480 | tf_op jit(solution)/shard_map/reshape | solution.py:56
  98.0 11.2 %convolution_bitcast_fusion.3 = f32[108,33540]{1,0:T(8,128)} fusion(bf16[128,33540]{0,1:T(8,128)(2,1)} %reshape.173, bf16[108,128]{1,0:T(8,128)(2,1)S(1)} %reshape.174), kind=kOutput, calls=%fused_computation.35 | convolution fusion | flops 927313920 | bytes 23103168 | tf_op jit(solution)/shard_map/dot_general | solution.py:54
  109.2 20.5 %reshape.175 = f32[9,12,130,258]{3,2,1,0:T(8,128)} reshape(f32[108,33540]{1,0:T(8,128)} %convolution_bitcast_fusion.3) | data formatting | bytes 28978560 | tf_op jit(solution)/shard_map/reshape | solution.py:59
  129.6 10.4 fusion.17
  140.2 3.0 collective-permute-start.8
  145.1 13.3 %collective-permute-done.8 = bf16[24,112,256]{2,1,0:T(8,128)(2,1)S(1)} collective-permute-done((bf16[24,112,256]{2,1,0:T(8,128)(2,1)S(1)}, bf16[24,112,256]{2,1,0:T(8,128)(2,1)S(1)}, u32[]{:S(2)}, u32[]{:S(2)}) %collective-permute-start.8) | collective-permute-done | bytes 1376288 | tf_op jit(solution)/shard_map/ppermute | solution.py:18
  158.4 4.4 collective-permute-done.9
  163.9 2.5 pad_maximum_fusion.2
  166.4 6.4 copy.37
  172.8 6.3 collective-permute-start.10
  182.6 84.4 %collective-permute-done.10 = bf16[24,352,224]{1,2,0:T(8,128)(2,1)} collective-permute-done((bf16[24,352,224]{1,2,0:T(8,128)(2,1)}, bf16[24,352,224]{1,2,0:T(8,128)(2,1)}, u32[]{:S(2)}, u32[]{:S(2)}) %collective-permute-start.10) | collective-permute-done | bytes 3784736 | tf_op jit(solution)/shard_map/ppermute | solution.py:30
  267.0 6.4 copy.38
  273.3 14.7 %pad_maximum_fusion.1 = bf16[24,352,480]{2,1,0:T(8,128)(2,1)} fusion(bf16[24,352,224]{2,1,0:T(8,128)(2,1)} %copy.38, bf16[24,112,256]{2,1,0:T(8,128)(2,1)} %copy-done.7, bf16[12,128,256]{2,1,0:T(8,128)(2,1)S(1)} %get-tuple-element.246, bf16[12,128,256]{2,1,0:T(8,128)(2,1)S(1)} %multiply_convert_fusion.3, bf16[24,112,256]{2,1,0:T(8,128)(2,1)S(1)} %collective-permute-done.8), kind=kLoop, calls=%fused_computation.38 | loop fusion | flops 40550400 | bytes 16220160 | tf_op jit(solution)/shard_map/concatenate | solution.py:148
  288.1 4.8 broadcast_in_dim.12
  292.9 242.8 %while.16 = (s32[]{:T(128)}, f32[13,352,480]{2,1,0:T(8,128)}, s32[]{:T(128)}, s32[16]{0:T(128)S(1)}, s32[16,2]{0,1:T(2,128)S(1)}, /*index=5*/s32[]{:T(128)}, s32...) while((s32[]{:T(128)}, f32[13,352,480]{2,1,0:T(8,128)}, ...), condition=%wide.wide.region_4.5_spmd, body=%wide.wide.region_2.4_spmd.sunk | while | flops 5921261568 | bytes 324800064 | solution.py:161
  298.3 4.8 constant_dynamic-slice_fusion.8
  303.2 3.0 slice_dynamic-update-slice_fusion.30
  306.2 2.9 slice_dynamic-update-slice_fusion.31
  309.1 3.2 slice_dynamic-update-slice_fusion.32
  312.3 2.8 slice_dynamic-update-slice_fusion.33
  315.2 6.3 constant_dynamic-update-slice_fusion.4
  321.5 2.7 slice_dynamic-update-slice_fusion.34
  324.2 15.6 %slice_dynamic-update-slice_fusion.35 = bf16[216,224,224]{2,1,0:T(8,128)(2,1)} fusion(bf16[216,224,224]{2,1,0:T(8,128)(2,1)} %slice_dynamic-update-slice_fusion.34, bf16[24,224,224]{2,1,0:T(8,128)(2,1)S(1)} %constant_dynamic-slice_fusion.8), kind=kLoop, calls=%fused_computation.20.clone.clone.1 | loop fusion | bytes 5160960 | tf_op jit(solution)/shard_map/while
  339.7 2.9 slice_dynamic-update-slice_fusion.36
  342.6 3.2 slice_dynamic-update-slice_fusion.37
  345.9 46.0 %reshape.194 = bf16[216,50176]{1,0:T(8,128)(2,1)} reshape(bf16[216,224,224]{2,1,0:T(8,128)(2,1)} %slice_dynamic-update-slice_fusion.37) | data formatting | bytes 43352064 | tf_op jit(solution)/shard_map/while/body/reshape | solution.py:44
  391.8 18.6 %convert_reduce_fusion.4 = (f32[128]{0:T(128)S(1)}, bf16[128,50176]{0,1:T(8,128)(2,1)}) fusion(bf16[216,50176]{1,0:T(8,128)(2,1)} %reshape.194, bf16[128,216]{0,1:T(8,128)(2,1)S(1)} %bitcast.138), kind=kOutput, calls=%fused_computation.5.clone.clone.1 | convolution fusion | flops 2819489792 | bytes 34576896 | tf_op jit(solution)/shard_map/while/body/dot_general | solution.py:46
  410.6 10.2 multiply_convert_fusion.6
  420.8 7.7 pad.194
  428.4 17.2 %reshape.195 = bf16[128,51076]{0,1:T(8,128)(2,1)} reshape(bf16[128,226,226]{0,2,1:T(8,128)(2,1)} %pad.194) | data formatting | bytes 26150912 | tf_op jit(solution)/shard_map/while/body/reshape | solution.py:56
  445.7 15.9 %convolution_bitcast_fusion.9 = f32[108,51076]{1,0:T(8,128)} fusion(bf16[128,51076]{0,1:T(8,128)(2,1)} %reshape.195, bf16[108,128]{1,0:T(8,128)(2,1)S(1)} %get-tuple-element.474), kind=kOutput, calls=%fused_computation.clone.clone.1 | convolution fusion | flops 1412149248 | bytes 35167936 | tf_op jit(solution)/shard_map/while/body/dot_general | solution.py:54
  461.5 27.5 %reshape.196 = f32[9,12,226,226]{3,2,1,0:T(8,128)} reshape(f32[108,51076]{1,0:T(8,128)} %convolution_bitcast_fusion.9) | data formatting | bytes 44129664 | tf_op jit(solution)/shard_map/while/body/reshape | solution.py:59
  489.0 10.5 fusion.61
  499.6 3.2 maximum_add_fusion.3
  502.8 28.1 %dynamic_update_slice.8 = f32[13,352,480]{2,1,0:T(8,128)} dynamic-update-slice(f32[13,352,480]{2,1,0:T(8,128)} %get-tuple-element.442, f32[13,224,224]{2,1,0:T(8,128)S(1)} %maximum_add_fusion.3, s32[]{:T(128)} %constant.162.clone.1..sunk, s32[]{:T(128)S(6)} %select_n.54, s32[]{:T(128)S(6)} %select_n.55) | dynamic-update-slice | bytes 5218308 | tf_op jit(solution)/shard_map/while/body/dynamic_update_slice | solution.py:108
  535.8 2.6 slice.474
  538.4 3.5 copy.39
  543.7 4.9 slice.333
  548.6 482.5 %collective-permute-done.11 = bf16[13,352,224]{1,2,0:T(8,128)(2,1)} collective-permute-done((bf16[13,352,224]{1,2,0:T(8,128)(2,1)}, bf16[13,352,224]{1,2,0:T(8,128)(2,1)}, u32[]{:S(2)}, u32[]{:S(2)}) %collective-permute-start.11) | collective-permute-done | bytes 2050080 | tf_op jit(solution)/shard_map/ppermute | solution.py:30
  1031.2 3.9 copy.40
  1035.1 4.9 convert_add_fusion
  1040.0 30.2 %scatter-add.10 = f32[13,352,256]{2,1,0:T(8,128)} dynamic-update-slice(f32[13,352,256]{2,1,0:T(8,128)} %slice.333, f32[13,352,224]{2,1,0:T(8,128)} %convert_add_fusion, s32[]{:T(128)} %constant.162.clone.1, s32[]{:T(128)} %constant.162.clone.1, s32[]{:T(128)} %constant.162.clone.1) | dynamic-update-slice | bytes 8200196 | tf_op jit(solution)/shard_map/scatter-add | solution.py:166
  1070.2 2.7 convert.10
  1075.0 2.4 collective-permute-start.13
  1077.7 5.8 collective-permute-done.12
  1083.4 4.4 collective-permute-done.13
  1089.9 2.2 fusion.15
  (78 shorter events, 21.7 us)
Async XLA Ops:
  0.6 30.8 %copy-start.3 = (bf16[12,128,256]{2,1,0:T(8,128)(2,1)S(1)}, bf16[12,128,256]{2,1,0:T(8,128)(2,1)}, u32[]{:S(2)}) copy-start(bf16[12,128,256]{2,1,0:T(8,128)(2,1)} %param.20) | copy-start | bytes 2359300
  0.6 17.6 %copy-start.10 = (bf16[9,128,12]{1,2,0:T(8,128)(2,1)S(1)}, bf16[9,128,12]{1,2,0:T(8,128)(2,1)}, u32[]{:S(2)}) copy-start(bf16[9,128,12]{1,2,0:T(8,128)(2,1)} %param.23) | copy-start | bytes 82948
  1.6 5.6 collective-permute-start
  5.3 5.0 collective-permute-start.1
  11.9 13.3 %collective-permute-start.3 = (bf16[12,130,1]{2,1,0:T(8,128)(2,1)S(1)}, bf16[12,130,1]{2,1,0:T(8,128)(2,1)S(1)}, u32[]{:S(2)}, u32[]{:S(2)}) collective-permute-start(bf16[12,130,1]{2,1,0:T(8,128)(2,1)S(1)} %get-tuple-element.264), channel_id=1, source_target_pairs={{1,0},{2,1},{3,2},{4,3},{5,4},{6,5},{7,6},{8,7},{9,8},{10,9},{11,1... | collective-permute-start | bytes 9368 | tf_op jit(solution)/shard_map/ppermute | solution.py:20
  16.4 15.0 %collective-permute-start.2 = (bf16[12,130,1]{2,1,0:T(8,128)(2,1)S(1)}, bf16[12,130,1]{2,1,0:T(8,128)(2,1)S(1)}, u32[]{:S(2)}, u32[]{:S(2)}) collective-permute-start(bf16[12,130,1]{2,1,0:T(8,128)(2,1)S(1)} %get-tuple-element.265), channel_id=1, source_target_pairs={{0,1},{1,2},{2,3},{3,4},{4,5},{5,6},{6,7},{7,8},{8,9},{9,10},{10,1... | collective-permute-start | bytes 9368 | tf_op jit(solution)/shard_map/ppermute | solution.py:18
  54.8 9.6 copy-start
  54.8 6.5 collective-permute-start.4
  58.7 5.6 collective-permute-start.5
  61.3 10.5 copy-start.4
  61.3 10.6 copy-start.11
  64.4 7.6 collective-permute-start.6
  66.3 6.8 collective-permute-start.7
  140.2 18.2 %collective-permute-start.8 = (bf16[24,112,256]{2,1,0:T(8,128)(2,1)S(1)}, bf16[24,112,256]{2,1,0:T(8,128)(2,1)S(1)}, u32[]{:S(2)}, u32[]{:S(2)}) collective-permute-start(bf16[24,112,256]{2,1,0:T(8,128)(2,1)S(1)} %get-tuple-element.262), channel_id=1, source_target_pairs={{0,16},{16,32},{32,48},{48,64},{64,80},{80,96},{96,112},{1,17},{17... | collective-permute-start | bytes 4128776 | tf_op jit(solution)/shard_map/ppermute | solution.py:18
  143.2 19.6 %collective-permute-start.9 = (bf16[24,112,256]{2,1,0:T(8,128)(2,1)S(1)}, bf16[24,112,256]{2,1,0:T(8,128)(2,1)S(1)}, u32[]{:S(2)}, u32[]{:S(2)}) collective-permute-start(bf16[24,112,256]{2,1,0:T(8,128)(2,1)S(1)} %get-tuple-element.263), channel_id=1, source_target_pairs={{16,0},{32,16},{48,32},{64,48},{80,64},{96,80},{112,96},{17,1},{33... | collective-permute-start | bytes 4128776 | tf_op jit(solution)/shard_map/ppermute | solution.py:20
  162.8 1.1 copy-start.7
  166.4 13.4 %copy-start.12 = (bf16[9,12,128]{2,1,0:T(8,128)(2,1)S(1)}, bf16[9,12,128]{2,1,0:T(8,128)(2,1)}, u32[]{:S(2)}) copy-start(bf16[9,12,128]{2,1,0:T(8,128)(2,1)} %param.28) | copy-start | bytes 82948
  166.4 13.4 %copy-start.9 = (s32[224,224]{1,0:T(8,128)S(1)}, s32[224,224]{1,0:T(8,128)}, u32[]{:S(2)}) copy-start(s32[224,224]{1,0:T(8,128)} %param.31) | copy-start | bytes 602116
  166.4 14.1 %copy-start.13 = (s32[1,16,2]{1,2,0:T(2,128)S(1)}, s32[1,16,2]{1,2,0:T(2,128)}, u32[]{:S(2)}) copy-start(s32[1,16,2]{1,2,0:T(2,128)} %param.29) | copy-start | bytes 388
  172.8 94.1 %collective-permute-start.10 = (bf16[24,352,224]{1,2,0:T(8,128)(2,1)}, bf16[24,352,224]{1,2,0:T(8,128)(2,1)}, u32[]{:S(2)}, u32[]{:S(2)}) collective-permute-start(bf16[24,352,224]{1,2,0:T(8,128)(2,1)} %copy.37), channel_id=1, source_target_pairs={{1,0},{2,1},{3,2},{4,3},{5,4},{6,5},{7,6},{8,7},{9,8},{10,9},{11,1... | collective-permute-start | bytes 11354120 | tf_op jit(solution)/shard_map/ppermute | solution.py:30
  288.1 4.9 copy-start.8
  288.1 4.9 copy-start.15
  288.1 4.9 copy-start.16
  293.9 12.3 %copy-start.17 = (s32[16]{0:T(128)}, s32[16]{0:T(128)S(1)}, u32[]{:S(2)}) copy-start(s32[16]{0:T(128)S(1)} %get-tuple-element.464) | copy-start | bytes 196 | tf_op jit(solution)/shard_map/while
  461.5 27.5 %copy-start.2 = (f32[224,224]{1,0:T(8,128)S(1)}, f32[224,224]{1,0:T(8,128)}, u32[]{:S(2)}) copy-start(f32[224,224]{1,0:T(8,128)} %get-tuple-element.473) | copy-start | bytes 602116 | tf_op jit(solution)/shard_map/while
  502.8 28.1 %copy-start.14 = (s32[1,16,2]{1,2,0:T(2,128)S(1)}, s32[1,16,2]{1,2,0:T(2,128)}, u32[]{:S(2)}) copy-start(s32[1,16,2]{1,2,0:T(2,128)} %get-tuple-element.525) | copy-start | bytes 388 | tf_op jit(solution)/shard_map/while
  502.8 28.1 %copy-start.18 = (s32[16]{0:T(128)S(1)}, s32[16]{0:T(128)}, u32[]{:S(2)}) copy-start(s32[16]{0:T(128)} %copy-done.17) | copy-start | bytes 196 | tf_op jit(solution)/shard_map/while
  541.8 489.3 %collective-permute-start.11 = (bf16[13,352,224]{1,2,0:T(8,128)(2,1)}, bf16[13,352,224]{1,2,0:T(8,128)(2,1)}, u32[]{:S(2)}, u32[]{:S(2)}) collective-permute-start(bf16[13,352,224]{1,2,0:T(8,128)(2,1)} %copy.39), channel_id=1, source_target_pairs={{0,1},{1,2},{2,3},{3,4},{4,5},{5,6},{6,7},{7,8},{8,9},{9,10},{10,1... | collective-permute-start | bytes 6150152 | tf_op jit(solution)/shard_map/ppermute | solution.py:30
  1070.2 7.3 copy-start.1
  1073.0 10.4 collective-permute-start.12
  1075.0 12.9 %collective-permute-start.13 = (bf16[13,112,256]{2,1,0:T(8,128)(2,1)S(1)}, bf16[13,112,256]{2,1,0:T(8,128)(2,1)S(1)}, u32[]{:S(2)}, u32[]{:S(2)}) collective-permute-start(bf16[13,112,256]{2,1,0:T(8,128)(2,1)S(1)} %get-tuple-element.261), channel_id=1, source_target_pairs={{16,0},{32,16},{48,32},{64,48},{80,64},{96,80},{112,96},{17,1},{33... | collective-permute-start | bytes 2236424 | tf_op jit(solution)/shard_map/ppermute | solution.py:20
  1088.0 1.4 copy-start.5
  1088.0 1.9 copy-start.6
where the time goes:
time: 1110 us; the launch traced here: 1090 us
  waiting for transfers between devices  615 us (55%)
  local copies, waits for them, and re-layouts  290 us (26%)
  other arithmetic  74.3 us (7%)
  matrix products  58.6 us (5%)
  starting transfers between devices  42.6 us (4%)
    ppermute x2, waiting for transfers between devices, passed_along(): return lax.ppermute(block, axis, route)  567 us
    reshape x2, local copies, waits for them, and re-layouts, conv_spread(): flat = flat.reshape(9, outputs, full_rows, full_cols)  47.9 us
    reshape x1, local copies, waits for them, and re-layouts, conv_gather(): stacked = stacked.reshape(9 * channels, height * breadth)  46 us
    while x16, local copies, waits for them, and re-layouts  39.5 us
    reshape x2, local copies, waits for them, and re-layouts, conv_spread(): padded.reshape(channels, full_rows * full_cols)  30.4 us
    scatter-add x1, local copies, waits for them, and re-layouts, body(): totals = totals.at[:, :, :patch].add(incoming)  30.2 us
    dynamic_update_slice x1, local copies, waits for them, and re-layouts, add_patch(): return lax.dynamic_update_slice(totals, old + term, start)  28.1 us
    dot_general x2, matrix products, conv_spread(): jnp.dot(weight.reshape(9 * outputs, channels), padded.reshape(channels, f...  27.1 us
  transfers between devices with their start and end apart: 14, of which 11 were waited for; matrix products, arithmetic and copies ran while one was open for 1% of the time, Pallas kernels for 0%

commit v1 on v0

v1 whole, which is shorter than its diff:
```python
import functools

import jax
import jax.numpy as jnp
from jax import lax
from jax.experimental import pallas as pl
from jax.experimental.pallas import tpu as pltpu
from jax.sharding import PartitionSpec as P

sigma_data = 0.5
step_ratio = 0.6

HALO = 4
STRIDE = 272
GROUP = 8
CHUNK = GROUP * STRIDE
PAD = 384
FRONT = 544
NEG = -1e30
VMEM = 60 * 1024 * 1024
f32, bf16 = jnp.float32, jnp.bfloat16


def silu_half(t):
    return t + t * jnp.tanh(t)


def tap_offsets():
    return [(a - 1) * STRIDE + (b - 1) for a in range(3) for b in range(3)]


def regress_kernel(
    rows, patch, tile_r, tile_c,
    meta, order, tab_r, tab_c,
    coarse, latent, rowi, coli, r0v, c0v, w1, w2, w3, wring,
    first_out, mean_out, part_out, ring_out, strips_out,
    hidden, cond_a, cond_b, cond_c, colmask, sbuf, sem,
):
    chunks = rows // GROUP
    offs = tap_offsets()
    row_lo, row_hi, col_lo, col_hi, number = (meta[0], meta[1], meta[2], meta[3], meta[4])
    hidden[:, :PAD] = jnp.zeros((128, PAD), bf16)
    hidden[:, PAD + chunks * CHUNK :] = jnp.zeros((128, PAD), bf16)
    for ref in (cond_a, cond_b):
        ref[:, :PAD] = jnp.zeros((ref.shape[0], PAD), ref.dtype)
        ref[:, PAD + chunks * CHUNK :] = jnp.zeros((ref.shape[0], PAD), ref.dtype)
    cond_c[:FRONT, :] = jnp.zeros((FRONT, 128), f32)
    cond_c[FRONT + chunks * CHUNK :, :] = jnp.zeros((FRONT, 128), f32)

    @pl.loop(0, chunks)
    def _(k):
        base = pl.multiple_of(k * CHUNK, 128)
        wide = coarse[:, pl.ds(base, CHUNK + 2 * PAD)]
        stack = jnp.concatenate([wide[:, PAD + o : PAD + o + CHUNK] for o in offs], 0)
        t = jnp.dot(w1[...], stack, preferred_element_type=f32)
        row = rowi[...] + k * GROUP
        col = coli[...]
        inside = (row >= row_lo) & (row < row_hi) & (col >= col_lo) & (col < col_hi)
        keep = jnp.where(inside, 1.0, 0.0)[:1]
        hidden[:, pl.ds(base + PAD, CHUNK)] = (silu_half(t) * keep).astype(bf16)

    @pl.loop(0, chunks)
    def _(k):
        base = pl.multiple_of(k * CHUNK, 128)
        y = jnp.dot(w2[...], hidden[:, pl.ds(base, CHUNK + 2 * PAD)], preferred_element_type=f32)
        mean = None
        for t, o in enumerate(offs):
            term = y[16 * t : 16 * t + 16, PAD + o : PAD + o + CHUNK]
            mean = term if mean is None else mean + term
        mean_out[:, pl.ds(base, CHUNK)] = mean
        lat = latent[:, pl.ds(base + PAD, CHUNK)].astype(f32)
        mid = lat[8:] + mean[:8]
        cond_a[:, pl.ds(base + PAD, CHUNK)] = jnp.concatenate([lat[:8], mid], 0).astype(bf16)
        cond_b[:, pl.ds(base + PAD, CHUNK)] = mean[8:]
        full = jnp.concatenate([lat[:8], mid, mean[8:], jnp.zeros((104, CHUNK), f32)], 0)
        for j in range(CHUNK // 128):
            cond_c[pl.ds(base + FRONT + 128 * j, 128), :] = full[:, 128 * j : 128 * j + 128].T

    jcol = lax.broadcasted_iota(jnp.int32, (STRIDE, 128), 0)
    c0b = c0v[...]
    in_cols = (
        (jcol > c0b) & (jcol < c0b + (patch - 1)) & (jcol >= HALO) & (jcol < HALO + tile_c)
    )
    colmask[...] = jnp.where(in_cols, 1.0, 0.0).astype(bf16)
    part_out[...] = jnp.zeros_like(part_out)

    @pl.loop(0, chunks)
    def _(k):
        base = pl.multiple_of(k * CHUNK, 128)
        wa = cond_a[:, pl.ds(base, CHUNK + 2 * PAD)]
        wb = cond_b[:, pl.ds(base, CHUNK + 2 * PAD)]
        parts = [wa[:, PAD + o : PAD + o + CHUNK] for o in offs]
        for a in range(3):
            b8 = [wb[:, PAD + o : PAD + o + CHUNK] for o in offs[3 * a : 3 * a + 3]]
            parts.append(jnp.concatenate([b8[0], b8[1]], 0).astype(bf16))
            parts.append(jnp.concatenate([b8[2], b8[2]], 0).astype(bf16))
        stack = jnp.concatenate(parts, 0)
        t = jnp.dot(w3[...], stack, preferred_element_type=f32)
        first = silu_half(t).astype(bf16)
        first_out[:, pl.ds(base, CHUNK)] = first
        r0b = r0v[...]
        cm = colmask[...]
        masks = []
        for i in range(GROUP):
            row = k * GROUP + i
            keep = (
                (r0b < row) & (row < r0b + (patch - 1)) & (row >= HALO) & (row < HALO + tile_r)
            )
            masks.append(cm * jnp.where(keep, 1.0, 0.0).astype(bf16))
        part_out[...] += jnp.dot(first, jnp.concatenate(masks, 0), preferred_element_type=f32)

    ring_out[...] = jnp.zeros_like(ring_out)

    def strip(start, count, stride, taps, valid_of):
        total = None
        for a, b in taps:
            where = start + (a - 1) * STRIDE + (b - 1)
            if stride == 1:
                cells = cond_c[pl.ds(where, count), :]
            else:
                cells = cond_c[pl.ds(where, count, stride=stride), :]
            cells = jnp.where(valid_of(a, b), cells, 0.0).astype(bf16)
            term = jnp.dot(cells, wring[3 * a + b], preferred_element_type=f32)
            total = term if total is None else total + term
        got = silu_half(total)
        if count % 16:
            got = jnp.concatenate([got, jnp.zeros((16 - count % 16, 128), f32)], 0)
        return got.astype(bf16)

    @pl.loop(0, number)
    def _(n):
        q = order[n]
        r0, c0 = tab_r[q], tab_c[q]
        r1, c1 = r0 + patch - 1, c0 + patch - 1
        j = lax.broadcasted_iota(jnp.int32, (STRIDE, 128), 0)
        i = lax.broadcasted_iota(jnp.int32, (rows, 128), 0)

        def add(value, weight):
            got = jnp.sum(value.astype(f32) * jnp.where(weight, 1.0, 0.0), 0, keepdims=True)
            ring_out[pl.ds(q, 1), :] += got

        for s, (r, height) in enumerate(((r0, (1, 2)), (r1, (0, 1)))):

            @pl.when((r >= HALO - 1) & (r <= HALO + tile_r))
            def _(s=s, r=r, height=height):
                value = strip(
                    FRONT + r * STRIDE, STRIDE, 1,
                    [(a, b) for a in height for b in range(3)],
                    lambda a, b: (j + (b - 1) >= c0) & (j + (b - 1) <= c1),
                )
                sbuf[s, :, :] = value
                own = (r >= HALO) & (r < HALO + tile_r)
                add(value, own & (j >= c0) & (j <= c1) & (j >= HALO) & (j < HALO + tile_c))

        for s, (c, breadth) in enumerate(((c0, (1, 2)), (c1, (0, 1)))):

            @pl.when((c >= HALO - 1) & (c <= HALO + tile_c))
            def _(s=s, c=c, breadth=breadth):
                value = strip(
                    FRONT + c, rows, STRIDE,
                    [(a, b) for a in range(3) for b in breadth],
                    lambda a, b: (i + (a - 1) >= r0) & (i + (a - 1) <= r1),
                )
                sbuf[2 + s, : value.shape[0], :] = value
                own = (c >= HALO) & (c < HALO + tile_c)
                add(value[:rows], own & (i > r0) & (i < r1) & (i >= HALO) & (i < HALO + tile_r))

        copy = pltpu.make_async_copy(sbuf, strips_out.at[n], sem)
        copy.start()
        copy.wait()


def patch_kernel(
    rows, patch, tile_r, tile_c,
    meta, order, tab_r, tab_c,
    first, strips, lift, weight, coli, ones, w4, w5,
    out,
    m, acc, sbuf, keep_row, keep_col, wcol, sem,
):
    chunks = rows // GROUP
    offs = tap_offsets()
    number = meta[4]
    wide = CHUNK + 2 * PAD
    tiles = wide // 128
    m[:FRONT, :] = jnp.zeros((FRONT, 128), f32)
    m[FRONT + chunks * CHUNK :, :] = jnp.zeros((FRONT, 128), f32)

    @pl.loop(0, chunks)
    def _(k):
        base = pl.multiple_of(k * CHUNK, 128)
        x = first[:, pl.ds(base, CHUNK)]
        y = lax.dot_general(x, w4[...], (((0,), (0,)), ((), ())), preferred_element_type=f32)
        m[pl.ds(base + FRONT, CHUNK), :] = y

    acc[...] = jnp.zeros_like(acc)

    @pl.loop(0, number)
    def _(n):
        q = order[n]
        r0, c0 = tab_r[q], tab_c[q]
        r1, c1 = r0 + patch - 1, c0 + patch - 1
        copy = pltpu.make_async_copy(strips.at[n], sbuf, sem)
        copy.start()
        copy.wait()
        half_lift = lift[pl.ds(q, 1), :]
        j = lax.broadcasted_iota(jnp.int32, (STRIDE, 128), 0)
        i = lax.broadcasted_iota(jnp.int32, (rows, 128), 0)

        def row_ok(r):
            return (r >= HALO - 1) & (r <= HALO + tile_r)

        def col_ok(c):
            return (c >= HALO - 1) & (c <= HALO + tile_c)

        def row_at(r):
            return pl.ds(FRONT + r * STRIDE, STRIDE)

        def col_at(c):
            return pl.ds(FRONT + c, rows, stride=STRIDE)

        cols = ((0, c0 - 1, None), (1, c0, 2), (2, c1, 3), (3, c1 + 1, None))
        rws = ((0, r0 - 1, None), (1, r0, 0), (2, r1, 1), (3, r1 + 1, None))
        for s, c, source in cols:

            @pl.when(col_ok(c))
            def _(s=s, c=c, source=source):
                keep_col[s, :, :] = m[col_at(c), :]
                if source is None:
                    m[col_at(c), :] = jnp.full((rows, 128), NEG, f32)
                else:
                    cells = sbuf[source, : -(-rows // 16) * 16, :]
                    got = jnp.dot(cells, w4[...], preferred_element_type=f32)[:rows]
                    m[col_at(c), :] = jnp.where((i >= r0) & (i <= r1), got, NEG)

        for s, r, source in rws:

            @pl.when(row_ok(r))
            def _(s=s, r=r, source=source):
                keep_row[s, :, :] = m[row_at(r), :]
                if source is None:
                    m[row_at(r), :] = jnp.full((STRIDE, 128), NEG, f32)
                else:
                    got = jnp.dot(sbuf[source], w4[...], preferred_element_type=f32)
                    m[row_at(r), :] = jnp.where((j >= c0) & (j <= c1), got, NEG)

        col = coli[...]
        wcol[...] = jnp.where((col >= c0) & (col <= c1), 1.0, 0.0)
        shift = r0 * STRIDE + c0

        @pl.loop(jnp.maximum(r0, HALO - 1) // GROUP, jnp.minimum(r1, HALO + tile_r) // GROUP + 1)
        def _(k):
            base = pl.multiple_of(k * CHUNK, 128)
            t = m[pl.ds(base + FRONT, CHUNK), :] + half_lift
            inner = silu_half(t).astype(bf16)
            y = lax.dot_general(
                w5[...], inner, (((1,), (1,)), ((), ())), preferred_element_type=f32
            )
            total = None
            for t, o in enumerate(offs):
                term = y[16 * t : 16 * t + 16]
                lead = PAD - o
                term = jnp.concatenate(
                    [jnp.zeros((16, lead), f32), term, jnp.zeros((16, wide - lead - CHUNK), f32)], 1
                )
                total = term if total is None else total + term
            lane = base - PAD - shift + WFRONT
            rem = lane % 128
            start = lane // 128
            blocks = weight[pl.ds(start, tiles + 1), :, :].reshape((tiles + 1) * 8, 128)
            rolled = pltpu.roll(blocks, (128 - rem) % 128, 1).reshape(tiles + 1, 8, 128)
            at = lax.broadcasted_iota(jnp.int32, (8, 128), 1)
            w8 = jnp.concatenate(
                [jnp.where(at < 128 - rem, rolled[x], rolled[x + 1]) for x in range(tiles)], 1
            )
            w8 = w8 * wcol[...]
            w16 = jnp.concatenate([w8, w8], 0)
            acc[:, pl.ds(base, wide)] += (total + ones[...]) * w16

        for s, r, source in rws[::-1]:

            @pl.when(row_ok(r))
            def _(s=s, r=r):
                m[row_at(r), :] = keep_row[s, :, :]

        for s, c, source in cols[::-1]:

            @pl.when(col_ok(c))
            def _(s=s, c=c):
                m[col_at(c), :] = keep_col[s, :, :]

    @pl.loop(0, chunks)
    def _(k):
        base = pl.multiple_of(k * CHUNK, 128)
        got = acc[:, pl.ds(base + PAD, CHUNK)]
        out[:, pl.ds(base, CHUNK)] = got / (1.0 + got[12:13])


WFRONT = 4096


def passed(block, axis, step):
    count = lax.axis_size(axis)
    route = [(i, i + step) for i in range(count) if 0 <= i + step < count]
    return lax.ppermute(block, axis, route)


def with_halo(cells, axis, dim, width):
    head = lax.slice_in_dim(cells, 0, width, axis=dim)
    tail = lax.slice_in_dim(cells, cells.shape[dim] - width, cells.shape[dim], axis=dim)
    return jnp.concatenate([passed(tail, axis, 1), cells, passed(head, axis, -1)], axis=dim)


def precondition(noise_level):
    level = noise_level[0]
    spread = level * level + sigma_data * sigma_data
    return (
        1.0 / jnp.sqrt(spread),
        sigma_data * sigma_data / spread,
        level * sigma_data / jnp.sqrt(spread),
    )


def body(
    coarse, latent, noise_level, reg_first, reg_second, den_first, den_middle, den_pool, den_last,
    anchors, patch_count, patch_weight,
):
    channels, tile_r, tile_c = latent.shape
    inputs = coarse.shape[0]
    patch = patch_weight.shape[0]
    rows = tile_r + 2 * HALO
    size = rows * STRIDE
    slab = lax.axis_index("slab")
    column = lax.axis_index("patch")
    scale_in, skip, scale_out = precondition(noise_level)

    both = jnp.concatenate([coarse, (scale_in * latent).astype(bf16)], 0)
    both = with_halo(with_halo(both, "slab", 1, HALO), "patch", 2, HALO)
    both = jnp.pad(both, ((0, 0), (0, 0), (0, STRIDE - both.shape[2])))
    both = both.reshape(inputs + channels, size)
    coarse_flat = jnp.pad(both[:inputs], ((0, 16 - inputs), (PAD, PAD)))
    latent_flat = jnp.pad(both[inputs:], ((0, 16 - channels), (PAD, PAD)))

    table = jnp.concatenate([anchors[0], jnp.broadcast_to(patch_count[:, None], (1, 2))], 0)
    tables = jnp.stack([passed(table, "slab", 1), table, passed(table, "slab", -1)], 0)
    per_slab = anchors.shape[1]
    live = jnp.arange(per_slab)[None, :] < tables[:, per_slab, :1]
    tab_r = tables[:, :per_slab, 0] - slab * tile_r + HALO
    tab_c = tables[:, :per_slab, 1] - column * tile_c + HALO
    live = live & (tab_r < HALO + tile_r) & (tab_r + patch > HALO)
    live = (live & (tab_c < HALO + tile_c) & (tab_c + patch > HALO)).reshape(-1)
    far = 1 << 20
    entries = 3 * per_slab
    tab_r = jnp.where(live, tab_r.reshape(-1), far)
    tab_c = jnp.where(live, tab_c.reshape(-1), far)
    place = jnp.cumsum(live.astype(jnp.int32)) - 1
    number = jnp.sum(live.astype(jnp.int32))
    labels = jnp.arange(entries, dtype=jnp.int32)
    hit = live[None, :] & (place[None, :] == labels[:, None])
    order = jnp.sum(jnp.where(hit, labels[None, :], 0), 1)
    top = HALO - slab * tile_r
    left = HALO - column * tile_c
    meta = jnp.stack(
        [
            top, top + lax.axis_size("slab") * tile_r,
            left, left + lax.axis_size("patch") * tile_c, number,
        ]
    ).astype(jnp.int32)

    w1 = 0.5 * jnp.pad(jnp.transpose(reg_first, (1, 0, 2)), ((0, 0), (0, 0), (0, 16 - inputs)))
    w1 = w1.reshape(128, 144)
    w2 = jnp.pad(reg_second, ((0, 0), (4, 0), (0, 0))).reshape(144, 128)
    den = 0.5 * den_first
    main = jnp.transpose(den[:, :, :16], (1, 0, 2)).reshape(128, 144)
    rest = den[:, :, 16:]
    zero = jnp.zeros_like(rest[0])
    side = []
    for a in range(3):
        side += [rest[3 * a], rest[3 * a + 1], rest[3 * a + 2], zero]
    w3 = jnp.concatenate([main] + side, 1)
    wring = jnp.pad(jnp.transpose(den, (0, 2, 1)), ((0, 0), (0, 128 - 2 * channels), (0, 0)))
    w4 = (0.5 * den_middle).T
    w5 = jnp.pad(den_last, ((0, 0), (0, 4), (0, 0))).reshape(144, 128)

    flat = jnp.arange(CHUNK, dtype=jnp.int32)
    rowi = jnp.broadcast_to(flat // STRIDE, (8, CHUNK))
    coli = jnp.broadcast_to(flat % STRIDE, (8, CHUNK))
    lanes_r = jnp.pad(tab_r, (0, 128 - entries), constant_values=far)[None]
    lanes_c = jnp.pad(tab_c, (0, 128 - entries), constant_values=far)[None]

    smem = pl.BlockSpec(memory_space=pltpu.SMEM)
    vmem = pl.BlockSpec(memory_space=pltpu.VMEM)
    anyw = pl.BlockSpec(memory_space=pl.ANY)
    fixed = (rows, patch, tile_r, tile_c)
    params = pltpu.CompilerParams(vmem_limit_bytes=VMEM)
    first, mean, part, ring, strips = pl.pallas_call(
        functools.partial(regress_kernel, *fixed),
        in_specs=[smem] * 4 + [vmem] * 10,
        out_specs=[vmem, vmem, vmem, vmem, anyw],
        out_shape=[
            jax.ShapeDtypeStruct((128, size), bf16),
            jax.ShapeDtypeStruct((16, size), f32),
            jax.ShapeDtypeStruct((128, 128), f32),
            jax.ShapeDtypeStruct((entries, 128), f32),
            jax.ShapeDtypeStruct((entries, 4, STRIDE, 128), bf16),
        ],
        scratch_shapes=[
            pltpu.VMEM((128, size + 2 * PAD), bf16),
            pltpu.VMEM((16, size + 2 * PAD), bf16),
            pltpu.VMEM((8, size + 2 * PAD), f32),
            pltpu.VMEM((size + 2 * FRONT, 128), f32),
            pltpu.VMEM((STRIDE, 128), bf16),
            pltpu.VMEM((4, STRIDE, 128), bf16),
            pltpu.SemaphoreType.DMA,
        ],
        compiler_params=params,
        name="regress",
    )(
        meta, order, tab_r, tab_c,
        coarse_flat, latent_flat, rowi, coli, lanes_r, lanes_c, w1, w2, w3, wring,
    )

    sums = ring + part[:, :entries].T
    sums = sums + passed(sums, "patch", 1) + passed(sums, "patch", -1)
    sums = sums.reshape(3, per_slab, 128)
    owned = sums[1] + passed(sums[2], "slab", 1) + passed(sums[0], "slab", -1)
    sums = jnp.stack([passed(owned, "slab", 1), owned, passed(owned, "slab", -1)], 0)
    pooled = sums.reshape(entries, 128) / (patch * patch)
    lift = 0.5 * jnp.dot(pooled, den_pool.astype(f32).T, precision=lax.Precision.HIGHEST)

    weight = jnp.pad(patch_weight.astype(f32), ((0, 0), (0, STRIDE - patch))).reshape(-1)
    weight = jnp.pad(weight, (WFRONT, 4096 + 128))
    weight = jnp.broadcast_to(weight.reshape(-1, 1, 128), (weight.shape[0] // 128, 8, 128))
    wide = CHUNK + 2 * PAD
    spot = jnp.arange(wide, dtype=jnp.int32)
    coli_wide = jnp.broadcast_to((spot - PAD + 2 * STRIDE) % STRIDE, (8, wide))
    ones = jnp.where(
        (jnp.arange(16)[:, None] >= 12) & (spot[None] >= PAD) & (spot[None] < PAD + CHUNK), 1.0, 0.0
    )
    blended = pl.pallas_call(
        functools.partial(patch_kernel, *fixed),
        in_specs=[smem] * 4 + [vmem, anyw] + [vmem] * 6,
        out_specs=vmem,
        out_shape=jax.ShapeDtypeStruct((16, size), f32),
        scratch_shapes=[
            pltpu.VMEM((size + 2 * FRONT, 128), f32),
            pltpu.VMEM((16, size + 2 * PAD), f32),
            pltpu.VMEM((4, STRIDE, 128), bf16),
            pltpu.VMEM((4, STRIDE, 128), f32),
            pltpu.VMEM((4, rows, 128), f32),
            pltpu.VMEM((8, wide), f32),
            pltpu.SemaphoreType.DMA,
        ],
        compiler_params=params,
        name="patches",
    )(
        meta, order, tab_r, tab_c,
        first, strips, lift, weight, coli_wide, ones, w4, w5,
    )

    def tile_of(flat):
        return flat.reshape(-1, rows, STRIDE)[:, HALO : HALO + tile_r, HALO : HALO + tile_c]

    blended = tile_of(blended[:channels])
    mean = tile_of(mean[4:])
    denoised = skip * latent + scale_out * blended
    next_state = latent + (step_ratio - 1.0) * (latent - denoised)
    return (next_state, mean + denoised)


def solution(mesh):
    return jax.shard_map(
        body,
        mesh=mesh,
        in_specs=(
            P(None, "slab", "patch"), P(None, "slab", "patch"),
            P(), P(), P(), P(), P(), P(), P(),
            P("slab", None, None), P("slab"), P(),
        ),
        out_specs=(P(None, "slab", "patch"), P(None, "slab", "patch")),
        check_vma=False,
    )
```

time: 1110 us -> 238 us (0.21)
  the two profiles are of different devices: /device:TPU:99 before, /device:TPU:25 now
where the time goes in v1:
time: 238 us; the launch traced here: 237 us
  Pallas kernels  149 us (63%)
  local copies, waits for them, and re-layouts  31 us (13%)
  starting transfers between devices  29.5 us (12%)
  other arithmetic  16.6 us (7%)
  waiting for transfers between devices  7.92 us (3%)
  between operations  2.74 us (1%)
    pallas_call x1, Pallas kernels, body(): pl.pallas_call(functools.partial(patch_kernel, *fixed), in_specs=[smem] *...  83.8 us
    pallas_call x1, Pallas kernels, body(): pl.pallas_call(functools.partial(regress_kernel, *fixed), in_specs=[smem]...  64.9 us
    ppermute x12, starting transfers between devices, passed(): return lax.ppermute(block, axis, route)  29.5 us
    ppermute x12, waiting for transfers between devices, passed(): return lax.ppermute(block, axis, route)  7.92 us
    reshape x2, local copies, waits for them, and re-layouts, tile_of(): flat.reshape(-1, rows, STRIDE)[:, HALO:HALO + tile_r, HALO:HALO + tile_c]  6.14 us
    concatenate x2, other arithmetic, with_halo(): jnp.concatenate([passed(tail, axis, 1), cells, passed(head, axis, -1)], a...  5.98 us
    add x1, other arithmetic, body(): return (next_state, mean + denoised)  5.04 us
  transfers between devices with their start and end apart: 12, of which 3 were waited for; matrix products, arithmetic and copies ran while one was open for 8% of the time, Pallas kernels for 0%

profile of v1, /device:TPU:25, one launch (start us, length us, event | category | flops | bytes accessed | tf_op | source)
XLA Modules:
  0.0 237.2 jit_solution(13935508744246430041)
XLA Ops:
  1.4 0.7 concatenate.15
  2.1 2.6 %collective-permute-start.1 = (s32[17,2]{0,1:T(2,128)S(1)}, s32[17,2]{0,1:T(2,128)S(1)}, u32[]{:S(2)}, u32[]{:S(2)}) collective-permute-start(s32[17,2]{0,1:T(2,128)S(1)} %concatenate.15), channel_id=1, source_target_pairs={{16,0},{32,16},{48,32},{64,48},{80,64},{96,80},{112,96},{17,1},{33... | collective-permute-start | bytes 416 | tf_op jit(solution)/shard_map/ppermute | solution.py:304
  4.7 3.0 %collective-permute-start = (s32[17,2]{0,1:T(2,128)S(1)}, s32[17,2]{0,1:T(2,128)S(1)}, u32[]{:S(2)}, u32[]{:S(2)}) collective-permute-start(s32[17,2]{0,1:T(2,128)S(1)} %concatenate.15), channel_id=1, source_target_pairs={{0,16},{16,32},{32,48},{48,64},{64,80},{80,96},{96,112},{1,17},{17... | collective-permute-start | bytes 416 | tf_op jit(solution)/shard_map/ppermute | solution.py:304
  8.5 1.6 multiply_convert_fusion
  10.1 2.4 %collective-permute-start.2 = (bf16[24,4,256]{2,0,1:T(8,128)(2,1)S(1)}, bf16[24,4,256]{2,0,1:T(8,128)(2,1)S(1)}, u32[]{:S(2)}, u32[]{:S(2)}) collective-permute-start(bf16[24,4,256]{2,0,1:T(8,128)(2,1)S(1)} %copy.105), channel_id=1, source_target_pairs={{0,16},{16,32},{32,48},{48,64},{64,80},{80,96},{96,112},{1,17},{17... | collective-permute-start | bytes 147464 | tf_op jit(solution)/shard_map/ppermute | solution.py:304
  12.5 1.9 collective-permute-start.3
  14.6 0.1 copy.114
  14.7 0.1 copy.115
  14.9 0.1 copy.116
  15.0 0.1 copy.117
  15.1 0.1 copy.118
  15.2 0.1 copy.119
  15.4 0.1 copy.120
  15.5 0.1 copy.121
  15.6 0.1 copy.122
  15.9 0.7 copy.123.w1
  16.6 0.8 pad.50.wring
  17.4 0.6 pad.49
  18.2 0.8 and_select_fusion.ones
  19.0 0.8 concatenate.19.w3
  19.9 0.2 slice_reduce_fusion
  21.4 0.7 convert_reduce_fusion
  22.1 0.6 select_reduce_fusion.order
  22.8 1.1 pad_maximum_fusion
  23.9 0.4 fusion.31
  24.3 0.5 copy.109
  24.8 3.2 %collective-permute-start.4 = (bf16[24,136,4]{1,0,2:T(8,128)(2,1)S(1)}, bf16[24,136,4]{1,0,2:T(8,128)(2,1)S(1)}, u32[]{:S(2)}, u32[]{:S(2)}) collective-permute-start(bf16[24,136,4]{1,0,2:T(8,128)(2,1)S(1)} %copy.109), channel_id=1, source_target_pairs={{0,1},{1,2},{2,3},{3,4},{4,5},{5,6},{6,7},{7,8},{8,9},{9,10},{10,1... | collective-permute-start | bytes 78344 | tf_op jit(solution)/shard_map/ppermute | solution.py:304
  28.0 0.5 copy.110
  28.6 2.3 collective-permute-start.5
  30.9 0.6 pad_bitcast_fusion.1
  31.4 1.3 stack.51.meta
  32.7 0.5 copy.111
  33.2 3.0 %collective-permute-done.5 = bf16[24,136,4]{1,0,2:T(8,128)(2,1)S(1)} collective-permute-done((bf16[24,136,4]{1,0,2:T(8,128)(2,1)S(1)}, bf16[24,136,4]{1,0,2:T(8,128)(2,1)S(1)}, u32[]{:S(2)}, u32[]{:S(2)}) %collective-permute-start.5) | collective-permute-done | bytes 26144 | tf_op jit(solution)/shard_map/ppermute | solution.py:304
  36.2 0.5 copy.112
  36.7 4.9 %fusion.7 = bf16[24,136,272]{2,1,0:T(8,128)(2,1)S(1)} fusion(bf16[24,136,4]{2,1,0:T(8,128)(2,1)S(1)} %copy.112, bf16[24,136,4]{2,1,0:T(8,128)(2,1)S(1)} %copy.111, bf16[24,4,256]{2,1,0:T(4,128)(2,1)S(1)} %copy.108, bf16[24,4,256]{2,1,0:T(4,128)(2,1)S(1)} %copy.107, bf16[12,128,256]{2,1,0:T(8,128)(2,1)S(1)} %multiply_convert_fusion, ...), kind=kLoop, calls=%fused_computation.8 | loop fusion | flops 16868352 | bytes 3499008 | tf_op jit(solution)/shard_map/concatenate | solution.py:310
  41.6 0.3 fusion.30
  41.9 2.2 slice.108
  44.0 2.4 %pad.44.coarse = bf16[16,37760]{1,0:T(8,128)(2,1)} pad(bf16[12,36992]{1,0:T(8,128)(2,1)} %slice.108, bf16[]{:T(256)} %constant.90.clone.1), padding=0_4x384_384 | pad | bytes 2096130 | tf_op jit(solution)/shard_map/jit(_pad)/pad | solution.py:340
  46.4 1.2 slice.110
  47.6 1.1 pad.45.latent
  48.7 0.6 broadcast_in_dim.67.rowi
  49.4 0.6 broadcast_in_dim.68.coli
  50.0 64.9 %regress.1 = (bf16[128,36992]{1,0:T(8,128)(2,1)}, f32[16,36992]{1,0:T(8,128)}, f32[128,128]{1,0:T(8,128)}, f32[48,128]{1,0:T(8,128)}, bf16[48,4,272,128]{3,2,1,0:T(8,128)(2,1)}) custom-call(s32[5]{0:T(128)} %stack.51.meta, s32[48]{0:T(128)} %select_reduce_fusion.order, s32[48]{0:T(128)} %copy-done.10, s32[48]{0:T(128)} %copy-done.9, ...), custom_call_target="tpu_custom_call" | custom-call | tf_op jit(solution)/shard_map/regress/pallas_call | solution.py:395
  114.9 0.9 copy.124
  115.8 0.7 fusion.12
  116.6 1.9 collective-permute-start.6
  118.5 3.4 %collective-permute-start.7 = (f32[48,128]{1,0:T(8,128)S(1)}, f32[48,128]{1,0:T(8,128)S(1)}, u32[]{:S(2)}, u32[]{:S(2)}) collective-permute-start(f32[48,128]{1,0:T(8,128)S(1)} %fusion.12), channel_id=1, source_target_pairs={{1,0},{2,1},{3,2},{4,3},{5,4},{6,5},{7,6},{8,7},{9,8},{10,9},{11,1... | collective-permute-start | bytes 73736 | tf_op jit(solution)/shard_map/ppermute | solution.py:304
  121.9 0.6 multiply_bitcast_fusion.w4
  122.6 0.3 reshape.282
  122.9 2.3 collective-permute-done.7
  125.2 1.9 collective-permute-start.8
  127.1 2.4 %collective-permute-start.9 = (f32[16,128]{1,0:T(8,128)S(1)}, f32[16,128]{1,0:T(8,128)S(1)}, u32[]{:S(2)}, u32[]{:S(2)}) collective-permute-start(f32[16,128]{1,0:T(8,128)S(1)} %get-tuple-element.44), channel_id=1, source_target_pairs={{16,0},{32,16},{48,32},{64,48},{80,64},{96,80},{112,96},{17,1},{33... | collective-permute-start | bytes 24584 | tf_op jit(solution)/shard_map/ppermute | solution.py:304
  129.6 2.5 %collective-permute-done.9 = f32[16,128]{1,0:T(8,128)S(1)} collective-permute-done((f32[16,128]{1,0:T(8,128)S(1)}, f32[16,128]{1,0:T(8,128)S(1)}, u32[]{:S(2)}, u32[]{:S(2)}) %collective-permute-start.9) | collective-permute-done | bytes 8224 | tf_op jit(solution)/shard_map/ppermute | solution.py:304
  132.1 1.9 collective-permute-start.10
  134.0 2.6 %collective-permute-start.11 = (f32[16,128]{1,0:T(8,128)S(1)}, f32[16,128]{1,0:T(8,128)S(1)}, u32[]{:S(2)}, u32[]{:S(2)}) collective-permute-start(f32[16,128]{1,0:T(8,128)S(1)} %fusion.24), channel_id=1, source_target_pairs={{16,0},{32,16},{48,32},{64,48},{80,64},{96,80},{112,96},{17,1},{33... | collective-permute-start | bytes 24584 | tf_op jit(solution)/shard_map/ppermute | solution.py:304
  136.7 0.6 pad.53
  137.4 1.8 slice.127
  139.3 2.4 reshape.285
  141.6 0.8 convolution_multiply_fusion.lift
  142.4 1.5 broadcast_in_dim.73.weight
  144.0 0.6 broadcast_in_dim.74.coli
  144.6 83.8 %patches.1 = f32[16,36992]{1,0:T(8,128)} custom-call(s32[5]{0:T(128)} %stack.51.meta, s32[48]{0:T(128)} %select_reduce_fusion.order, s32[48]{0:T(128)} %copy-done.10, s32[48]{0:T(128)} %copy-done.9, bf16[128,36992]{1,0:T(8,128)(2,1)} %get-tuple-element.7.first, bf16[48,4,272,128]{3,2,1,0:T(8,128)(2,1)} %get-tuple-element.8.strips, ...), custom_call_target="tpu_custom_call" | custom-call | tf_op jit(solution)/shard_map/patches/pallas_call | solution.py:439
  228.4 3.8 %reshape.284 = f32[12,136,272]{2,1,0:T(8,128)} reshape(f32[12,36992]{1,0:T(8,128)} %bitcast.78) | data formatting | bytes 3551232 | tf_op jit(solution)/shard_map/reshape | solution.py:461
  232.2 5.0 %slice_add_fusion = (f32[12,128,256]{2,1,0:T(8,128)}, f32[12,128,256]{2,1,0:T(8,128)}) fusion(f32[12,136,272]{2,1,0:T(8,128)S(1)} %copy-done.2, f32[12,136,272]{2,1,0:T(8,128)} %reshape.284, f32[12,128,256]{2,1,0:T(8,128)} %param.13, f32[]{:T(128)} %bitcast.1, f32[]{:T(128)} %bitcast), kind=kLoop, calls=%fused_computation.13 | loop fusion | flops 2752512 | bytes 7864328 | tf_op jit(solution)/shard_map/add | solution.py:467
  (78 shorter events, 1.9 us)
Async XLA Ops:
  0.6 141.0 %copy-start = (bf16[128,128]{1,0:T(8,128)(2,1)S(1)}, bf16[128,128]{1,0:T(8,128)(2,1)}, u32[]{:S(2)}) copy-start(bf16[128,128]{1,0:T(8,128)(2,1)} %param.19) | copy-start | bytes 98308
  0.6 13.9 %copy-start.11 = (s32[1,16,2]{1,2,0:T(2,128)S(1)}, s32[1,16,2]{1,2,0:T(2,128)}, u32[]{:S(2)}) copy-start(s32[1,16,2]{1,2,0:T(2,128)} %param.21) | copy-start | bytes 388
  0.7 9.4 %copy-start.1 = (bf16[12,128,256]{2,1,0:T(8,128)(2,1)S(1)}, bf16[12,128,256]{2,1,0:T(8,128)(2,1)}, u32[]{:S(2)}) copy-start(bf16[12,128,256]{2,1,0:T(8,128)(2,1)} %param.12) | copy-start | bytes 2359300
  0.7 13.8 %copy-start.4 = (bf16[9,128,24]{1,2,0:T(8,128)(2,1)S(1)}, bf16[9,128,24]{1,2,0:T(8,128)(2,1)}, u32[]{:S(2)}) copy-start(bf16[9,128,24]{1,2,0:T(8,128)(2,1)} %param.17) | copy-start | bytes 165892
  2.1 17.7 %collective-permute-start.1 = (s32[17,2]{0,1:T(2,128)S(1)}, s32[17,2]{0,1:T(2,128)S(1)}, u32[]{:S(2)}, u32[]{:S(2)}) collective-permute-start(s32[17,2]{0,1:T(2,128)S(1)} %concatenate.15), channel_id=1, source_target_pairs={{16,0},{32,16},{48,32},{64,48},{80,64},{96,80},{112,96},{17,1},{33... | collective-permute-start | bytes 416 | tf_op jit(solution)/shard_map/ppermute | solution.py:304
  4.7 15.1 %collective-permute-start = (s32[17,2]{0,1:T(2,128)S(1)}, s32[17,2]{0,1:T(2,128)S(1)}, u32[]{:S(2)}, u32[]{:S(2)}) collective-permute-start(s32[17,2]{0,1:T(2,128)S(1)} %concatenate.15), channel_id=1, source_target_pairs={{0,16},{16,32},{32,48},{48,64},{64,80},{80,96},{96,112},{1,17},{17... | collective-permute-start | bytes 416 | tf_op jit(solution)/shard_map/ppermute | solution.py:304
  8.3 7.5 %copy-start.5 = (bf16[9,128,12]{1,2,0:T(8,128)(2,1)S(1)}, bf16[9,128,12]{1,2,0:T(8,128)(2,1)}, u32[]{:S(2)}) copy-start(bf16[9,128,12]{1,2,0:T(8,128)(2,1)} %param.15) | copy-start | bytes 82948
  8.4 9.0 %copy-start.6 = (bf16[9,12,128]{2,1,0:T(8,128)(2,1)S(1)}, bf16[9,12,128]{2,1,0:T(8,128)(2,1)}, u32[]{:S(2)}) copy-start(bf16[9,12,128]{2,1,0:T(8,128)(2,1)} %param.16) | copy-start | bytes 82948
  8.4 9.6 %copy-start.8 = (bf16[128,128]{1,0:T(8,128)(2,1)S(1)}, bf16[128,128]{1,0:T(8,128)(2,1)}, u32[]{:S(2)}) copy-start(bf16[128,128]{1,0:T(8,128)(2,1)} %param.18) | copy-start | bytes 98308
  10.1 12.6 %collective-permute-start.2 = (bf16[24,4,256]{2,0,1:T(8,128)(2,1)S(1)}, bf16[24,4,256]{2,0,1:T(8,128)(2,1)S(1)}, u32[]{:S(2)}, u32[]{:S(2)}) collective-permute-start(bf16[24,4,256]{2,0,1:T(8,128)(2,1)S(1)} %copy.105), channel_id=1, source_target_pairs={{0,16},{16,32},{32,48},{48,64},{64,80},{80,96},{96,112},{1,17},{17... | collective-permute-start | bytes 147464 | tf_op jit(solution)/shard_map/ppermute | solution.py:304
  12.5 10.2 %collective-permute-start.3 = (bf16[24,4,256]{2,0,1:T(8,128)(2,1)S(1)}, bf16[24,4,256]{2,0,1:T(8,128)(2,1)S(1)}, u32[]{:S(2)}, u32[]{:S(2)}) collective-permute-start(bf16[24,4,256]{2,0,1:T(8,128)(2,1)S(1)} %copy.106), channel_id=1, source_target_pairs={{16,0},{32,16},{48,32},{64,48},{80,64},{96,80},{112,96},{17,1},{33... | collective-permute-start | bytes 147464 | tf_op jit(solution)/shard_map/ppermute | solution.py:304
  20.9 10.0 %copy-start.9 = (s32[48]{0:T(128)}, s32[48]{0:T(128)S(1)}, u32[]{:S(2)}) copy-start(s32[48]{0:T(128)S(1)} %get-tuple-element.14.tab_c) | copy-start | bytes 580
  20.9 10.0 %copy-start.10 = (s32[48]{0:T(128)}, s32[48]{0:T(128)S(1)}, u32[]{:S(2)}) copy-start(s32[48]{0:T(128)S(1)} %broadcast_select_fusion.1.tab_r) | copy-start | bytes 580
  24.8 7.9 %collective-permute-start.4 = (bf16[24,136,4]{1,0,2:T(8,128)(2,1)S(1)}, bf16[24,136,4]{1,0,2:T(8,128)(2,1)S(1)}, u32[]{:S(2)}, u32[]{:S(2)}) collective-permute-start(bf16[24,136,4]{1,0,2:T(8,128)(2,1)S(1)} %copy.109), channel_id=1, source_target_pairs={{0,1},{1,2},{2,3},{3,4},{4,5},{5,6},{6,7},{7,8},{8,9},{9,10},{10,1... | collective-permute-start | bytes 78344 | tf_op jit(solution)/shard_map/ppermute | solution.py:304
  28.6 7.6 %collective-permute-start.5 = (bf16[24,136,4]{1,0,2:T(8,128)(2,1)S(1)}, bf16[24,136,4]{1,0,2:T(8,128)(2,1)S(1)}, u32[]{:S(2)}, u32[]{:S(2)}) collective-permute-start(bf16[24,136,4]{1,0,2:T(8,128)(2,1)S(1)} %copy.110), channel_id=1, source_target_pairs={{1,0},{2,1},{3,2},{4,3},{5,4},{6,5},{7,6},{8,7},{9,8},{10,9},{11,1... | collective-permute-start | bytes 78344 | tf_op jit(solution)/shard_map/ppermute | solution.py:304
  47.6 74.9 %copy-start.3 = (s32[224,224]{1,0:T(8,128)S(1)}, s32[224,224]{1,0:T(8,128)}, u32[]{:S(2)}) copy-start(s32[224,224]{1,0:T(8,128)} %param.23) | copy-start | bytes 602116
  50.0 86.7 %copy-start.7 = (bf16[9,12,128]{2,1,0:T(8,128)(2,1)S(1)}, bf16[9,12,128]{2,1,0:T(8,128)(2,1)}, u32[]{:S(2)}) copy-start(bf16[9,12,128]{2,1,0:T(8,128)(2,1)} %param.20) | copy-start | bytes 82948
  116.6 6.3 %collective-permute-start.6 = (f32[48,128]{1,0:T(8,128)S(1)}, f32[48,128]{1,0:T(8,128)S(1)}, u32[]{:S(2)}, u32[]{:S(2)}) collective-permute-start(f32[48,128]{1,0:T(8,128)S(1)} %fusion.12), channel_id=1, source_target_pairs={{0,1},{1,2},{2,3},{3,4},{4,5},{5,6},{6,7},{7,8},{8,9},{9,10},{10,1... | collective-permute-start | bytes 73736 | tf_op jit(solution)/shard_map/ppermute | solution.py:304
  118.5 6.7 %collective-permute-start.7 = (f32[48,128]{1,0:T(8,128)S(1)}, f32[48,128]{1,0:T(8,128)S(1)}, u32[]{:S(2)}, u32[]{:S(2)}) collective-permute-start(f32[48,128]{1,0:T(8,128)S(1)} %fusion.12), channel_id=1, source_target_pairs={{1,0},{2,1},{3,2},{4,3},{5,4},{6,5},{7,6},{8,7},{9,8},{10,9},{11,1... | collective-permute-start | bytes 73736 | tf_op jit(solution)/shard_map/ppermute | solution.py:304
  125.2 4.4 %collective-permute-start.8 = (f32[16,128]{1,0:T(8,128)S(1)}, f32[16,128]{1,0:T(8,128)S(1)}, u32[]{:S(2)}, u32[]{:S(2)}) collective-permute-start(f32[16,128]{1,0:T(8,128)S(1)} %get-tuple-element.43), channel_id=1, source_target_pairs={{0,16},{16,32},{32,48},{48,64},{64,80},{80,96},{96,112},{1,17},{17... | collective-permute-start | bytes 24584 | tf_op jit(solution)/shard_map/ppermute | solution.py:304
  127.1 5.0 %collective-permute-start.9 = (f32[16,128]{1,0:T(8,128)S(1)}, f32[16,128]{1,0:T(8,128)S(1)}, u32[]{:S(2)}, u32[]{:S(2)}) collective-permute-start(f32[16,128]{1,0:T(8,128)S(1)} %get-tuple-element.44), channel_id=1, source_target_pairs={{16,0},{32,16},{48,32},{64,48},{80,64},{96,80},{112,96},{17,1},{33... | collective-permute-start | bytes 24584 | tf_op jit(solution)/shard_map/ppermute | solution.py:304
  132.1 9.5 %collective-permute-start.10 = (f32[16,128]{1,0:T(8,128)S(1)}, f32[16,128]{1,0:T(8,128)S(1)}, u32[]{:S(2)}, u32[]{:S(2)}) collective-permute-start(f32[16,128]{1,0:T(8,128)S(1)} %fusion.24), channel_id=1, source_target_pairs={{0,16},{16,32},{32,48},{48,64},{64,80},{80,96},{96,112},{1,17},{17... | collective-permute-start | bytes 24584 | tf_op jit(solution)/shard_map/ppermute | solution.py:304
  134.0 7.6 %collective-permute-start.11 = (f32[16,128]{1,0:T(8,128)S(1)}, f32[16,128]{1,0:T(8,128)S(1)}, u32[]{:S(2)}, u32[]{:S(2)}) collective-permute-start(f32[16,128]{1,0:T(8,128)S(1)} %fusion.24), channel_id=1, source_target_pairs={{16,0},{32,16},{48,32},{64,48},{80,64},{96,80},{112,96},{17,1},{33... | collective-permute-start | bytes 24584 | tf_op jit(solution)/shard_map/ppermute | solution.py:304
  228.4 3.8 %copy-start.2 = (f32[12,136,272]{2,1,0:T(8,128)S(1)}, f32[12,136,272]{2,1,0:T(8,128)}, u32[]{:S(2)}) copy-start(f32[12,136,272]{2,1,0:T(8,128)} %reshape.285) | copy-start | bytes 5326852

commit v2 on v1

v2 whole, which is shorter than its diff:
```python
import functools

import jax
import jax.numpy as jnp
from jax import lax
from jax.experimental import pallas as pl
from jax.experimental.pallas import tpu as pltpu
from jax.sharding import PartitionSpec as P

sigma_data = 0.5
step_ratio = 0.6

HALO = 4
STRIDE = 272
PLANES = 8
PAD = 384
FRONT = 544
STEP = 256
TILE = 512
COLUMN = 24
NEG = -1e30
VMEM = 60 * 1024 * 1024
f32, bf16 = jnp.float32, jnp.bfloat16


def lanes_of(rows):
    return -(-(rows // PLANES * STRIDE) // STEP) * STEP


def silu_half(t):
    return t + t * jnp.tanh(t)


def shifted(ref, base, step, depth):
    at = base + PAD
    edge = STRIDE // 128 * 128
    rest = STRIDE - edge
    mid = ref[:, pl.ds(at - 128, step + 256)]
    low = ref[(PLANES - 1) * depth :, pl.ds(at - edge - 128, step + 256)]
    high = ref[:depth, pl.ds(at + edge - 128, step + 256)]
    out = []
    for b in range(3):
        m = mid[:, 127 + b : 127 + b + step]
        rows = [low[:, 127 + b - rest : 127 + b - rest + step]]
        rows += [m[depth * i : depth * i + depth] for i in range(PLANES)]
        rows += [high[:, 127 + b + rest : 127 + b + rest + step]]
        out.append(rows)
    return out


def overlapped(parts):
    got = [parts[0][:96]]
    for a, b in zip(parts, parts[1:]):
        got.append(a[96:] + b[:96])
    return got + [parts[-1][96:]]


def combined(ref, base, step):
    at = base + PAD
    edge = STRIDE // 128 * 128
    rest = STRIDE - edge

    def columns(plane, start, move):
        total = None
        for b in range(3):
            row = (plane + 1) * 48 + b * 16
            block = ref[row : row + 16, pl.ds(start - 128, step + 256)]
            term = block[:, 127 + b + move : 127 + b + move + step]
            total = term if total is None else total + term
        return total

    planes = [columns(i, at, 0) for i in range(PLANES)]
    planes[-1] += columns(-1, at + edge, rest)
    planes[0] += columns(PLANES, at - edge, -rest)
    return planes


def regress_kernel(
    rows, patch, tile_r, tile_c,
    meta, order, tab_r, tab_c,
    coarse, latent, rowi, coli, r0v, c0v, w1, w2, w3, wrow, wcol,
    first_out, mean_out, part_out, ring_out, strips_out,
    sums, cond_a, cond_b, cond_c, sbuf, sem,
):
    size = lanes_of(rows)
    steps = size // STEP
    cells = size + 2 * FRONT
    groups = rows // PLANES
    row_lo, row_hi, col_lo, col_hi, number = (meta[0], meta[1], meta[2], meta[3], meta[4])
    for ref in (sums, cond_a, cond_b):
        ref[:, :PAD] = jnp.zeros((ref.shape[0], PAD), ref.dtype)
        ref[:, PAD + size :] = jnp.zeros((ref.shape[0], PAD), ref.dtype)
    cond_c[:FRONT, :] = jnp.zeros((FRONT, 128), f32)
    cond_c[FRONT + size : 2 * FRONT + size, :] = jnp.zeros((FRONT, 128), f32)
    cond_c[cells : cells + FRONT, :] = jnp.zeros((FRONT, 128), f32)
    cond_c[cells + FRONT + size :, :] = jnp.zeros((cond_c.shape[0] - cells - FRONT - size, 128), f32)

    @pl.loop(0, steps, unroll=4)
    def _(k):
        base = pl.multiple_of(k * STEP, 128)
        x = shifted(coarse, base, STEP, 16)
        row = rowi[:, pl.ds(base, STEP)]
        col = coli[:, pl.ds(base, STEP)]
        inside = (row >= row_lo) & (row < row_hi) & (col >= col_lo) & (col < col_hi)
        keep = jnp.where(inside, 1.0, 0.0)
        parts = []
        for pair in range(PLANES // 2):
            stack = jnp.concatenate(
                [x[b][2 * pair + r] for r in range(4) for b in range(3)], 0
            )
            h = silu_half(jnp.dot(w1[...], stack, preferred_element_type=f32))
            h = jnp.concatenate(
                [
                    h[:128] * keep[2 * pair : 2 * pair + 1],
                    h[128:] * keep[2 * pair + 1 : 2 * pair + 2],
                ],
                0,
            ).astype(bf16)
            parts.append(jnp.dot(w2[...], h, preferred_element_type=f32))
        sums[:, pl.ds(base + PAD, STEP)] = jnp.concatenate(overlapped(parts), 0)

    @pl.loop(0, steps, unroll=4)
    def _(k):
        base = pl.multiple_of(k * STEP, 128)
        means = combined(sums, base, STEP)
        lat = latent[:, pl.ds(base + PAD, STEP)].astype(f32)
        zero = jnp.zeros((8, STEP), f32)
        main, side, full = [], [], []
        for i, mean in enumerate(means):
            head = lat[16 * i : 16 * i + 8]
            mid = lat[16 * i + 8 : 16 * i + 16] + mean[:8]
            main += [head, mid]
            side.append(mean[8:])
            full += [head, mid, mean[8:], zero]
        mean_out[:, pl.ds(base, STEP)] = jnp.concatenate(means, 0)
        cond_a[:, pl.ds(base + PAD, STEP)] = jnp.concatenate(main, 0).astype(bf16)
        cond_b[:, pl.ds(base + PAD, STEP)] = jnp.concatenate(side, 0)
        for h in range(2):
            block = jnp.concatenate(full[16 * h : 16 * h + 16], 0)
            for j in range(STEP // 128):
                cond_c[pl.ds(base + h * cells + FRONT + 128 * j, 128), :] = block[
                    :, 128 * j : 128 * j + 128
                ].T

    part_out[...] = jnp.zeros_like(part_out)

    @pl.loop(0, steps, unroll=4)
    def _(k):
        base = pl.multiple_of(k * STEP, 128)
        xa = shifted(cond_a, base, STEP, 16)
        xb = shifted(cond_b, base, STEP, 8)
        left = [
            jnp.concatenate([xb[0][i], xb[1][i]], 0).astype(bf16) for i in range(PLANES + 2)
        ]
        right = [
            jnp.concatenate([xb[2][i], xb[2][min(i + 1, PLANES + 1)]], 0).astype(bf16)
            for i in range(PLANES + 2)
        ]
        group = base // STRIDE
        lane = lax.broadcasted_iota(jnp.int32, (STEP, 128), 0)
        split = (group + 1) * STRIDE - base
        later = lane >= split
        col = lane + base - group * STRIDE - jnp.where(later, STRIDE, 0)
        c0b, r0b = c0v[...], r0v[...]
        wanted = (
            (col > c0b) & (col < c0b + (patch - 1)) & (col >= HALO) & (col < HALO + tile_c)
        )
        now = jnp.where(wanted & (lane < split), 1.0, 0.0).astype(bf16)
        late = jnp.where(wanted & later, 1.0, 0.0).astype(bf16)

        def row_keep(row):
            keep = (
                (r0b < row) & (row < r0b + (patch - 1)) & (row >= HALO) & (row < HALO + tile_r)
            )
            return jnp.where(keep, 1.0, 0.0).astype(bf16)

        masks, firsts = [], []
        for i in range(PLANES):
            stack = jnp.concatenate(
                [xa[b][i + a] for a in range(3) for b in range(3)]
                + [left[i], left[i + 1], left[i + 2], right[i], right[i + 2]],
                0,
            )
            first = silu_half(jnp.dot(w3[...], stack, preferred_element_type=f32)).astype(bf16)
            first_out[128 * i : 128 * i + 128, pl.ds(base, STEP)] = first
            firsts.append(first)
            row = group * PLANES + i
            masks.append(now * row_keep(row) + late * row_keep(row + PLANES))
        part_out[...] += jnp.dot(
            jnp.concatenate(firsts, 1), jnp.concatenate(masks, 0), preferred_element_type=f32
        )

    ring_out[...] = jnp.zeros_like(ring_out)
    j = lax.broadcasted_iota(jnp.int32, (STRIDE, 128), 0)
    g = lax.broadcasted_iota(jnp.int32, (COLUMN, 128), 0)
    i = jnp.concatenate([g * PLANES + p for p in range(PLANES)], 0)
    live = jnp.concatenate([g < groups for p in range(PLANES)], 0)

    @pl.loop(0, number)
    def _(n):
        q = order[n]
        r0, c0 = tab_r[q], tab_c[q]
        r1, c1 = r0 + patch - 1, c0 + patch - 1

        def add(value, weight):
            got = jnp.sum(jnp.where(weight, value.astype(f32), 0.0), 0, keepdims=True)
            ring_out[pl.ds(q, 1), :] += got

        for s, (r, height) in enumerate(((r0, (1, 2)), (r1, (0, 1)))):

            @pl.when((r >= HALO - 1) & (r <= HALO + tile_r))
            def _(s=s, r=r, height=height):
                total = None
                for a in height:
                    at = r + a - 1
                    plane = at % PLANES
                    start = plane // 4 * cells + FRONT + at // PLANES * STRIDE
                    for b in range(3):
                        x = cond_c[pl.ds(start + b - 1, STRIDE), :]
                        x = jnp.where((j + (b - 1) >= c0) & (j + (b - 1) <= c1), x, 0.0)
                        term = jnp.dot(
                            x.astype(bf16), wrow[plane % 4, 3 * a + b], preferred_element_type=f32
                        )
                        total = term if total is None else total + term
                value = silu_half(total).astype(bf16)
                sbuf[STRIDE * s : STRIDE * s + STRIDE, :] = value
                own = (r >= HALO) & (r < HALO + tile_r)
                add(value, own & (j >= c0) & (j <= c1) & (j >= HALO) & (j < HALO + tile_c))

        for s, (c, breadth) in enumerate(((c0, (1, 2)), (c1, (0, 1)))):

            @pl.when((c >= HALO - 1) & (c <= HALO + tile_c))
            def _(s=s, c=c, breadth=breadth):
                total = None
                for b in breadth:

                    def at(h, g_move, b=b):
                        start = h * cells + FRONT + c + b - 1 + g_move * STRIDE
                        return cond_c[pl.ds(start, COLUMN, stride=STRIDE), :]

                    halves = [at(0, 0), at(1, 0)]
                    planes = [at(1, -1)[:, 96:]]
                    planes += [
                        halves[p // 4][:, p % 4 * 32 : p % 4 * 32 + 32] for p in range(PLANES)
                    ]
                    planes += [at(0, 1)[:, :32]]
                    for a in range(3):
                        x = jnp.concatenate(planes[a : a + PLANES], 0)
                        inside = (i + (a - 1) >= r0) & (i + (a - 1) <= r1)
                        x = jnp.where(inside[:, :32], x, 0.0).astype(bf16)
                        term = jnp.dot(x, wcol[3 * a + b], preferred_element_type=f32)
                        total = term if total is None else total + term
                value = silu_half(total).astype(bf16)
                lo = 2 * STRIDE + PLANES * COLUMN * s
                sbuf[lo : lo + PLANES * COLUMN, :] = value
                own = (c >= HALO) & (c < HALO + tile_c) & live
                add(value, own & (i > r0) & (i < r1) & (i >= HALO) & (i < HALO + tile_r))

        copy = pltpu.make_async_copy(sbuf, strips_out.at[n], sem)
        copy.start()
        copy.wait()


def patch_kernel(
    rows, patch, tile_r, tile_c,
    meta, order, tab_r, tab_c,
    first, strips, lift, weight, w4, w5,
    out,
    m, acc, sbuf, keep_row, keep_col, wbuf, sem,
):
    size = lanes_of(rows)
    steps = size // STEP
    groups = rows // PLANES
    number = meta[4]
    high = 2 * STRIDE
    tall = PLANES * COLUMN

    def fetch(n):
        return pltpu.make_async_copy(strips.at[n], sbuf.at[n % 2], sem.at[n % 2])

    @pl.when(number > 0)
    def _():
        fetch(0).start()

    @pl.loop(0, steps, unroll=2)
    def _(k):
        base = pl.multiple_of(k * STEP, 128)
        for i in range(PLANES):
            x = first[128 * i : 128 * i + 128, pl.ds(base, STEP)]
            y = lax.dot_general(x, w4[...], (((0,), (0,)), ((), ())), preferred_element_type=f32)
            m[pl.ds(base + i * size, STEP), :] = y

    acc[...] = jnp.zeros_like(acc)
    m[PLANES * size :, :] = jnp.zeros((TILE, 128), f32)
    j = lax.broadcasted_iota(jnp.int32, (STRIDE, 128), 0)
    g = lax.broadcasted_iota(jnp.int32, (COLUMN, 128), 0)
    lane = lax.broadcasted_iota(jnp.int32, (8, TILE), 1)
    ones = jnp.where(lax.broadcasted_iota(jnp.int32, (16, TILE), 0) >= 12, 1.0, 0.0)

    @pl.loop(0, number)
    def _(n):
        q = order[n]
        r0, c0 = tab_r[q], tab_c[q]
        r1, c1 = r0 + patch - 1, c0 + patch - 1
        slot = n % 2
        fetch(n).wait()

        @pl.when(n + 1 < number)
        def _():
            fetch(n + 1).start()

        half_lift = lift[pl.ds(q, 1), :]

        def row_ok(r):
            return (r >= HALO - 1) & (r <= HALO + tile_r)

        def col_ok(c):
            return (c >= HALO - 1) & (c <= HALO + tile_c)

        def row_at(r):
            return pl.ds(pl.multiple_of(r % PLANES * size + r // PLANES * STRIDE, 8), STRIDE)

        def col_at(c, i):
            return pl.ds(c + i * size, groups, stride=STRIDE)

        cols = ((0, c0 - 1, None), (1, c0, 0), (2, c1, 1), (3, c1 + 1, None))
        rws = ((0, r0 - 1, None), (1, r0, 0), (2, r1, 1), (3, r1 + 1, None))
        for s, c, source in cols:

            @pl.when(col_ok(c))
            def _(s=s, c=c, source=source):
                if source is not None:
                    strip = sbuf[slot, high + tall * source : high + tall * source + tall, :]
                    got = jnp.dot(strip, w4[...], preferred_element_type=f32)
                for i in range(PLANES):
                    keep_col[s, i, :groups, :] = m[col_at(c, i), :]
                    if source is None:
                        new = jnp.full((groups, 128), NEG, f32)
                    else:
                        row = g * PLANES + i
                        new = got[COLUMN * i : COLUMN * i + COLUMN]
                        new = jnp.where((row >= r0) & (row <= r1), new, NEG)[:groups]
                    m[col_at(c, i), :] = new

        for s, r, source in rws:

            @pl.when(row_ok(r))
            def _(s=s, r=r, source=source):
                keep_row[s, :, :] = m[row_at(r), :]
                if source is None:
                    m[row_at(r), :] = jnp.full((STRIDE, 128), NEG, f32)
                else:
                    strip = sbuf[slot, STRIDE * source : STRIDE * source + STRIDE, :]
                    got = jnp.dot(strip, w4[...], preferred_element_type=f32)
                    m[row_at(r), :] = jnp.where((j >= c0) & (j <= c1), got, NEG)

        top = r0 // PLANES
        phase = r0 - top * PLANES
        move = top * STRIDE + c0
        shifts = (move, move + STRIDE, jnp.where(phase == 0, move - STRIDE, move))
        clo, chi = jnp.maximum(c0, HALO - 1), jnp.minimum(c1, HALO + tile_c)
        glo = jnp.maximum(r0, HALO - 1) // PLANES
        ghi = jnp.minimum(r1, HALO + tile_r) // PLANES

        @pl.loop((glo * STRIDE + clo) // TILE, (ghi * STRIDE + chi) // TILE + 1)
        def _(k):
            base = pl.multiple_of(k * TILE, 128)
            col_start = base % STRIDE
            col = lane + col_start
            for _ in range((TILE + STRIDE - 2) // STRIDE):
                col = jnp.where(col >= STRIDE, col - STRIDE, col)
            for b in range(3):
                inside = (col - (b - 1) >= c0) & (col - (b - 1) <= c1)
                for v, shift in enumerate(shifts):
                    source = base - shift - (b - 1) + WFRONT
                    rem = source % 128
                    count = TILE // 128
                    blocks = weight[pl.ds(source // 128, count + 1), :, :]
                    blocks = blocks.reshape(8 * count + 8, 128)
                    rolled = pltpu.roll(blocks, (128 - rem) % 128, 1)
                    here = lane[:, :128] < 128 - rem
                    got = jnp.concatenate(
                        [
                            jnp.where(here, rolled[8 * x : 8 * x + 8], rolled[8 * x + 8 : 8 * x + 16])
                            for x in range(count)
                        ],
                        1,
                    )
                    wbuf[8 * (3 * v + b) : 8 * (3 * v + b) + 8, :] = jnp.where(inside, got, 0.0)
            pairs = []
            for pair in range(PLANES // 2):
                halves = []
                for i in (2 * pair, 2 * pair + 1):
                    t = m[pl.ds(base + i * size, TILE), :] + half_lift
                    halves.append(silu_half(t).astype(bf16))
                pairs.append(jnp.concatenate(halves, 1))
            y = lax.dot_general(
                w5[...], jnp.concatenate(pairs, 0), (((1,), (1,)), ((), ())),
                preferred_element_type=f32,
            )
            parts = overlapped([y[:, TILE * x : TILE * x + TILE] for x in range(PLANES // 2)])
            for i in range(-1, PLANES + 1):
                block = parts[(i + 1) // 2][(i + 1) % 2 * 48 : (i + 1) % 2 * 48 + 48]
                if i < 0:
                    version = 1
                elif i == PLANES:
                    version = 2
                else:
                    version = jnp.where(phase <= i, 0, 1)
                line = (i - phase) % PLANES
                for b in range(3):
                    term = block[16 * b : 16 * b + 16]
                    if b == 1 and 0 <= i < PLANES:
                        term = term + ones
                    w = wbuf[pl.ds(8 * (3 * version + b) + line, 1), :]
                    row = 48 * (i + 1) + 16 * b
                    acc[row : row + 16, pl.ds(base + PAD, TILE)] += term * w

        for s, r, source in rws[::-1]:

            @pl.when(row_ok(r))
            def _(s=s, r=r):
                m[row_at(r), :] = keep_row[s, :, :]

        for s, c, source in cols[::-1]:

            @pl.when(col_ok(c))
            def _(s=s, c=c):
                for i in range(PLANES):
                    m[col_at(c, i), :] = keep_col[s, i, :groups, :]

    @pl.loop(0, steps)
    def _(k):
        base = pl.multiple_of(k * STEP, 128)
        planes = combined(acc, base, STEP)
        out[:, pl.ds(base, STEP)] = jnp.concatenate([p / (1.0 + p[12:13]) for p in planes], 0)


WFRONT = 2048


def passed(block, axis, step):
    count = lax.axis_size(axis)
    route = [(i, i + step) for i in range(count) if 0 <= i + step < count]
    return lax.ppermute(block, axis, route)


def with_halo(cells, axis, dim, width):
    head = lax.slice_in_dim(cells, 0, width, axis=dim)
    tail = lax.slice_in_dim(cells, cells.shape[dim] - width, cells.shape[dim], axis=dim)
    return jnp.concatenate([passed(tail, axis, 1), cells, passed(head, axis, -1)], axis=dim)


def precondition(noise_level):
    level = noise_level[0]
    spread = level * level + sigma_data * sigma_data
    return (
        1.0 / jnp.sqrt(spread),
        sigma_data * sigma_data / spread,
        level * sigma_data / jnp.sqrt(spread),
    )


def specs():
    return (
        pl.BlockSpec(memory_space=pltpu.SMEM),
        pl.BlockSpec(memory_space=pltpu.VMEM),
        pl.BlockSpec(memory_space=pl.ANY),
    )


def run_regress(fixed, entries, *args):
    size = lanes_of(fixed[0])
    smem, vmem, anyw = specs()
    cells = size + 2 * FRONT
    return pl.pallas_call(
        functools.partial(regress_kernel, *fixed),
        in_specs=[smem] * 4 + [vmem] * 11,
        out_specs=[vmem, vmem, vmem, vmem, anyw],
        out_shape=[
            jax.ShapeDtypeStruct((PLANES * 128, size), bf16),
            jax.ShapeDtypeStruct((PLANES * 16, size), f32),
            jax.ShapeDtypeStruct((128, 128), f32),
            jax.ShapeDtypeStruct((entries, 128), f32),
            jax.ShapeDtypeStruct((entries, 2 * (STRIDE + PLANES * COLUMN), 128), bf16),
        ],
        scratch_shapes=[
            pltpu.VMEM((48 * (PLANES + 2), size + 2 * PAD), f32),
            pltpu.VMEM((16 * PLANES, size + 2 * PAD), bf16),
            pltpu.VMEM((8 * PLANES, size + 2 * PAD), f32),
            pltpu.VMEM((2 * cells + COLUMN * STRIDE - size + STRIDE, 128), f32),
            pltpu.VMEM((2 * (STRIDE + PLANES * COLUMN), 128), bf16),
            pltpu.SemaphoreType.DMA,
        ],
        compiler_params=pltpu.CompilerParams(vmem_limit_bytes=VMEM),
        name="regress",
    )(*args)


def run_patches(fixed, *args):
    rows = fixed[0]
    size = lanes_of(rows)
    smem, vmem, anyw = specs()
    return pl.pallas_call(
        functools.partial(patch_kernel, *fixed),
        in_specs=[smem] * 4 + [vmem, anyw] + [vmem] * 4,
        out_specs=vmem,
        out_shape=jax.ShapeDtypeStruct((PLANES * 16, size), f32),
        scratch_shapes=[
            pltpu.VMEM((PLANES * size + TILE, 128), f32),
            pltpu.VMEM((48 * (PLANES + 2), size + 2 * PAD), f32),
            pltpu.VMEM((2, 2 * (STRIDE + PLANES * COLUMN), 128), bf16),
            pltpu.VMEM((4, STRIDE, 128), f32),
            pltpu.VMEM((4, PLANES, COLUMN, 128), f32),
            pltpu.VMEM((72, TILE), f32),
            pltpu.SemaphoreType.DMA((2,)),
        ],
        compiler_params=pltpu.CompilerParams(vmem_limit_bytes=VMEM),
        name="patches",
    )(*args)


NEAR = [(di, dj) for di in range(-2, 3) for dj in range(-1, 2) if (di, dj) != (0, 0)]
MESH = pl.DeviceIdType.MESH


def neighbours(near, shape):
    me = (lax.axis_index("slab"), lax.axis_index("patch"))
    out = []
    for offset in near:
        at = tuple(a + d for a, d in zip(me, offset))
        there = (at[0] >= 0) & (at[0] < shape[0]) & (at[1] >= 0) & (at[1] < shape[1])
        out.append((there, at))
    return out


def greet(around):
    barrier = pltpu.get_barrier_semaphore()
    for there, at in around:

        @pl.when(there)
        def _(at=at):
            pl.semaphore_signal(barrier, inc=1, device_id=at, device_id_type=MESH)

    peers = jnp.int32(0)
    for there, at in around:
        peers = peers + there.astype(jnp.int32)
    pl.semaphore_wait(barrier, peers)


def pool_kernel(shape, per_slab, cells, part, ring, pool, lift, mine, got, send, recv):
    around = neighbours(NEAR, shape)
    greet(around)
    mine[...] = ring[...] + part[...].T[: 3 * per_slab]
    copies = []
    for x, (there, at) in enumerate(around):
        copy = pltpu.make_async_remote_copy(
            src_ref=mine, dst_ref=got.at[len(NEAR) - 1 - x],
            send_sem=send.at[x], recv_sem=recv.at[len(NEAR) - 1 - x],
            device_id=at, device_id_type=MESH,
        )
        copies.append(copy)

        @pl.when(there)
        def _(copy=copy):
            copy.start()

    lift[...] = mine[...]
    for x, (there, at) in enumerate(around):
        di = NEAR[x][0]

        @pl.when(there)
        def _(x=x, di=di):
            copies[len(NEAR) - 1 - x].wait_recv()
            for d in range(3):
                e = d - di
                if 0 <= e < 3:
                    lift[per_slab * d : per_slab * d + per_slab, :] += got[
                        x, per_slab * e : per_slab * e + per_slab, :
                    ]

    for x, (there, at) in enumerate(around):

        @pl.when(there)
        def _(x=x):
            copies[x].wait_send()

    lift[...] = 0.5 * lax.dot_general(
        lift[...] / cells, pool[...], (((1,), (1,)), ((), ())),
        precision=lax.Precision.HIGHEST, preferred_element_type=f32,
    )


def run_pool(shape, per_slab, cells, *args):
    vmem = specs()[1]
    entries = 3 * per_slab
    return pl.pallas_call(
        functools.partial(pool_kernel, shape, per_slab, cells),
        in_specs=[vmem] * 3,
        out_specs=vmem,
        out_shape=jax.ShapeDtypeStruct((entries, 128), f32),
        scratch_shapes=[
            pltpu.VMEM((entries, 128), f32),
            pltpu.VMEM((len(NEAR), entries, 128), f32),
            pltpu.SemaphoreType.DMA((len(NEAR),)),
            pltpu.SemaphoreType.DMA((len(NEAR),)),
        ],
        compiler_params=pltpu.CompilerParams(collective_id=1, has_side_effects=True),
        name="pool",
    )(*args)


def body(
    coarse, latent, noise_level, reg_first, reg_second, den_first, den_middle, den_pool, den_last,
    anchors, patch_count, patch_weight,
):
    channels, tile_r, tile_c = latent.shape
    inputs = coarse.shape[0]
    patch = patch_weight.shape[0]
    rows = tile_r + 2 * HALO
    size = lanes_of(rows)
    groups = rows // PLANES
    used = groups * STRIDE
    slab = lax.axis_index("slab")
    column = lax.axis_index("patch")
    scale_in, skip, scale_out = precondition(noise_level)

    both = jnp.concatenate([coarse, (scale_in * latent).astype(bf16)], 0)
    both = with_halo(with_halo(both, "slab", 1, HALO), "patch", 2, HALO)
    both = jnp.pad(both, ((0, 0), (0, 0), (0, STRIDE - both.shape[2])))
    both = both.reshape(inputs + channels, groups, PLANES, STRIDE).transpose(2, 0, 1, 3)
    both = both.reshape(PLANES, inputs + channels, used)

    def planes_of(part):
        part = jnp.pad(part, ((0, 0), (0, 16 - part.shape[1]), (PAD, PAD + size - used)))
        return part.reshape(PLANES * 16, size + 2 * PAD)

    coarse_flat = planes_of(both[:, :inputs])
    latent_flat = planes_of(both[:, inputs:])

    table = jnp.concatenate([anchors[0], jnp.broadcast_to(patch_count[:, None], (1, 2))], 0)
    tables = jnp.stack([passed(table, "slab", 1), table, passed(table, "slab", -1)], 0)
    per_slab = anchors.shape[1]
    live = jnp.arange(per_slab)[None, :] < tables[:, per_slab, :1]
    tab_r = tables[:, :per_slab, 0] - slab * tile_r + HALO
    tab_c = tables[:, :per_slab, 1] - column * tile_c + HALO
    live = live & (tab_r < HALO + tile_r) & (tab_r + patch > HALO)
    live = (live & (tab_c < HALO + tile_c) & (tab_c + patch > HALO)).reshape(-1)
    far = 1 << 20
    entries = 3 * per_slab
    tab_r = jnp.where(live, tab_r.reshape(-1), far)
    tab_c = jnp.where(live, tab_c.reshape(-1), far)
    place = jnp.cumsum(live.astype(jnp.int32)) - 1
    number = jnp.sum(live.astype(jnp.int32))
    labels = jnp.arange(entries, dtype=jnp.int32)
    hit = live[None, :] & (place[None, :] == labels[:, None])
    order = jnp.sum(jnp.where(hit, labels[None, :], 0), 1)
    top = HALO - slab * tile_r
    left = HALO - column * tile_c
    meta = jnp.stack(
        [
            top, top + lax.axis_size("slab") * tile_r,
            left, left + lax.axis_size("patch") * tile_c, number,
        ]
    ).astype(jnp.int32)

    def gather_pair(weight):
        taps = jnp.pad(jnp.transpose(weight, (1, 0, 2)), ((0, 0), (0, 0), (0, 16 - weight.shape[2])))
        taps = taps.reshape(128, 144)
        return jnp.concatenate(
            [jnp.pad(taps, ((0, 0), (0, 48))), jnp.pad(taps, ((0, 0), (48, 0)))], 0
        )

    def spread_pair(weight, front):
        taps = jnp.pad(weight, ((0, 0), (front, 16 - front - weight.shape[1]), (0, 0)))
        taps = taps.reshape(3, 48, 128)[::-1].reshape(144, 128)
        return jnp.concatenate(
            [jnp.pad(taps, ((0, 48), (0, 0))), jnp.pad(taps, ((48, 0), (0, 0)))], 1
        )

    w1 = gather_pair(0.5 * reg_first)
    w2 = spread_pair(reg_second, 4)
    den = 0.5 * den_first
    main = jnp.transpose(den[:, :, :16], (1, 0, 2)).reshape(128, 144)
    rest = den[:, :, 16:]
    side = [rest[t] for t in (0, 1, 3, 4, 6, 7, 2, 5, 8)] + [jnp.zeros_like(rest[0])]
    w3 = jnp.concatenate([main] + side, 1)
    wcol = jnp.pad(jnp.transpose(den, (0, 2, 1)), ((0, 0), (0, 32 - 2 * channels), (0, 0)))
    wrow = jnp.stack([jnp.pad(wcol, ((0, 0), (32 * u, 96 - 32 * u), (0, 0))) for u in range(4)], 0)
    w4 = (0.5 * den_middle).T
    w5 = spread_pair(den_last, 0)

    flat = jnp.arange(size, dtype=jnp.int32)
    rowi = PLANES * (flat // STRIDE)[None] + jnp.arange(PLANES, dtype=jnp.int32)[:, None]
    coli = jnp.broadcast_to(flat % STRIDE, (PLANES, size))
    lanes_r = jnp.pad(tab_r, (0, 128 - entries), constant_values=far)[None]
    lanes_c = jnp.pad(tab_c, (0, 128 - entries), constant_values=far)[None]

    fixed = (rows, patch, tile_r, tile_c)
    first, mean, part, ring, strips = run_regress(
        fixed, entries,
        meta, order, tab_r, tab_c,
        coarse_flat, latent_flat, rowi, coli, lanes_r, lanes_c, w1, w2, w3, wrow, wcol,
    )

    shape = (lax.axis_size("slab"), lax.axis_size("patch"))
    lift = run_pool(shape, per_slab, patch * patch, part, ring, den_pool.astype(f32))

    weight = jnp.pad(patch_weight.astype(f32), ((0, 0), (0, STRIDE - patch)))
    weight = weight.reshape(patch // PLANES, PLANES, STRIDE).transpose(1, 0, 2)
    weight = weight.reshape(PLANES, patch // PLANES * STRIDE)
    end = -weight.shape[1] % 128
    weight = jnp.pad(weight, ((0, 0), (WFRONT, end + WFRONT)))
    weight = weight.reshape(PLANES, -1, 128).transpose(1, 0, 2)
    blended = run_patches(
        fixed, meta, order, tab_r, tab_c, first, strips, lift, weight, w4, w5
    )

    def tile_of(flat):
        planes = flat.reshape(PLANES, 16, size)[:, :, :used].reshape(PLANES, 16, groups, STRIDE)
        whole = planes.transpose(1, 2, 0, 3).reshape(16, rows, STRIDE)
        return whole[:, HALO : HALO + tile_r, HALO : HALO + tile_c]

    blended = tile_of(blended)[:channels]
    mean = tile_of(mean)[4:]
    denoised = skip * latent + scale_out * blended
    next_state = latent + (step_ratio - 1.0) * (latent - denoised)
    return (next_state, mean + denoised)


def solution(mesh):
    return jax.shard_map(
        body,
        mesh=mesh,
        in_specs=(
            P(None, "slab", "patch"), P(None, "slab", "patch"),
            P(), P(), P(), P(), P(), P(), P(),
            P("slab", None, None), P("slab"), P(),
        ),
        out_specs=(P(None, "slab", "patch"), P(None, "slab", "patch")),
        check_vma=False,
    )
```

time: 238 us -> 216 us (0.908)
  the two profiles are of different devices: /device:TPU:25 before, /device:TPU:22 now
where the time goes in v2:
time: 216 us
  Pallas kernels  128 us (59%)
  local copies, waits for them, and re-layouts  45.3 us (21%)
  other arithmetic  22.6 us (10%)
  starting transfers between devices  16.4 us (8%)
  between operations  2.75 us (1%)
    pallas_call x1, Pallas kernels, run_patches(): pl.pallas_call(functools.partial(patch_kernel, *fixed), in_specs=[smem] *...  65.5 us
    pallas_call x1, Pallas kernels, run_regress(): pl.pallas_call(functools.partial(regress_kernel, *fixed), in_specs=[smem]...  51.4 us
    ppermute x6, starting transfers between devices, passed(): return lax.ppermute(block, axis, route)  16.4 us
    pallas_call x1, Pallas kernels, run_pool(): pl.pallas_call(functools.partial(pool_kernel, shape, per_slab, cells), in...  10.8 us
    transpose x2, local copies, waits for them, and re-layouts, tile_of(): whole = planes.transpose(1, 2, 0, 3).reshape(16, rows, STRIDE)  10.5 us
    squeeze x10, local copies, waits for them, and re-layouts, body(): rest[t]  6.42 us
    reshape x2, local copies, waits for them, and re-layouts, tile_of(): flat.reshape(PLANES, 16, size)[:, :, :used]  6.19 us
    transpose x1, other arithmetic, body(): both.reshape(inputs + channels, groups, PLANES, STRIDE)  4.92 us
  transfers between devices with their start and end apart: 6, of which 1 were waited for; matrix products, arithmetic and copies ran while one was open for 13% of the time, Pallas kernels for 0%

profile of v2, /device:TPU:22, one launch (start us, length us, event | category | flops | bytes accessed | tf_op | source)
XLA Modules:
  0.0 215.6 jit_solution(5725265135651459559)
XLA Ops:
  1.4 1.3 concatenate.24
  2.7 2.2 %collective-permute-start.1 = (s32[17,2]{0,1:T(2,128)}, s32[17,2]{0,1:T(2,128)}, u32[]{:S(2)}, u32[]{:S(2)}) collective-permute-start(s32[17,2]{0,1:T(2,128)} %concatenate.24), channel_id=1, source_target_pairs={{16,0},{32,16},{48,32},{64,48},{80,64},{96,80},{112,96},{17,1},{33... | collective-permute-start | bytes 416 | tf_op jit(solution)/shard_map/ppermute | solution.py:445
  4.8 2.6 %collective-permute-start = (s32[17,2]{0,1:T(2,128)}, s32[17,2]{0,1:T(2,128)}, u32[]{:S(2)}, u32[]{:S(2)}) collective-permute-start(s32[17,2]{0,1:T(2,128)} %concatenate.24), channel_id=1, source_target_pairs={{0,16},{16,32},{32,48},{48,64},{64,80},{80,96},{96,112},{1,17},{17... | collective-permute-start | bytes 416 | tf_op jit(solution)/shard_map/ppermute | solution.py:445
  8.2 1.6 multiply_convert_fusion
  9.8 0.7 pad_maximum_fusion.3
  10.5 1.9 collective-permute-start.2
  12.4 3.6 %collective-permute-start.3 = (bf16[24,4,256]{2,1,0:T(4,128)(2,1)}, bf16[24,4,256]{2,1,0:T(4,128)(2,1)S(1)}, u32[]{:S(2)}, u32[]{:S(2)}) collective-permute-start(bf16[24,4,256]{2,1,0:T(4,128)(2,1)} %get-tuple-element.31), channel_id=1, source_target_pairs={{16,0},{32,16},{48,32},{64,48},{80,64},{96,80},{112,96},{17,1},{33... | collective-permute-start | bytes 147464 | tf_op jit(solution)/shard_map/ppermute | solution.py:445
  16.1 0.6 fusion.22
  16.8 0.5 pad_bitcast_fusion.8
  17.4 0.7 copy.115
  18.1 0.7 copy.116
  18.8 0.7 copy.117
  19.5 0.7 copy.118
  20.2 0.7 copy.119
  20.9 0.7 copy.120
  21.6 0.7 copy.121
  22.4 0.7 copy.122
  23.1 0.7 copy.123
  23.9 0.2 pad_bitcast_fusion.5
  24.3 0.7 fusion.19.w1
  25.1 0.7 iota_add_fusion.rowi
  25.8 0.6 fusion.20.w2
  26.4 0.6 convert_element_type.63.pool
  27.1 1.0 convert_element_type.64
  28.1 0.2 reshape.309
  28.4 0.8 pad_bitcast_fusion.weight
  29.2 0.8 pad.99
  30.0 0.7 fusion.21.w5
  30.7 0.9 copy.125
  31.5 0.6 multiply_bitcast_fusion.1.w4
  32.2 1.2 pad_maximum_fusion.1.wrow
  33.5 0.8 concatenate.30.w3
  34.3 0.7 pad_add_fusion
  35.0 0.2 slice_reduce_fusion
  36.0 0.5 broadcast_select_fusion.1.tab_r
  37.0 0.8 convert_reduce_fusion
  37.8 0.6 select_reduce_fusion.order
  38.5 1.1 pad_maximum_fusion
  39.5 0.4 fusion.37
  39.9 0.5 copy.107
  40.5 3.2 %collective-permute-start.4 = (bf16[24,136,4]{1,0,2:T(8,128)(2,1)S(1)}, bf16[24,136,4]{1,0,2:T(8,128)(2,1)S(1)}, u32[]{:S(2)}, u32[]{:S(2)}) collective-permute-start(bf16[24,136,4]{1,0,2:T(8,128)(2,1)S(1)} %copy.107), channel_id=1, source_target_pairs={{0,1},{1,2},{2,3},{3,4},{4,5},{5,6},{6,7},{7,8},{8,9},{9,10},{10,1... | collective-permute-start | bytes 78344 | tf_op jit(solution)/shard_map/ppermute | solution.py:445
  43.7 0.5 copy.108
  44.2 2.8 %collective-permute-start.5 = (bf16[24,136,4]{1,0,2:T(8,128)(2,1)S(1)}, bf16[24,136,4]{1,0,2:T(8,128)(2,1)S(1)}, u32[]{:S(2)}, u32[]{:S(2)}) collective-permute-start(bf16[24,136,4]{1,0,2:T(8,128)(2,1)S(1)} %copy.108), channel_id=1, source_target_pairs={{1,0},{2,1},{3,2},{4,3},{5,4},{6,5},{7,6},{8,7},{9,8},{10,9},{11,1... | collective-permute-start | bytes 78344 | tf_op jit(solution)/shard_map/ppermute | solution.py:445
  47.1 0.5 pad_bitcast_fusion.6
  47.6 1.4 stack.54.meta
  49.0 0.5 copy.109
  49.4 0.8 collective-permute-done.5
  50.2 0.5 copy.110
  50.7 4.9 %fusion.8 = bf16[8,24,17,272]{3,0,2,1:T(8,128)(2,1)S(1)} fusion(bf16[24,136,4]{2,1,0:T(8,128)(2,1)S(1)} %copy.110, bf16[24,136,4]{2,1,0:T(8,128)(2,1)S(1)} %copy.109, bf16[24,4,256]{2,1,0:T(4,128)(2,1)S(1)} %collective-permute-done.3, bf16[24,4,256]{2,1,0:T(4,128)(2,1)S(1)} %collective-permute-done.2, bf16[12,128,256]{2,1,0:T(8,128)(2,1)S(1)} %multiply_convert_fusion, ...), kind=kLoop, calls=%fused_computation.11 | loop fusion | flops 16868352 | bytes 3499008 | tf_op jit(solution)/shard_map/transpose | solution.py:631
  55.6 0.6 copy.111
  56.2 3.1 %reshape.301 = bf16[8,24,4624]{2,1,0:T(8,128)(2,1)} reshape(bf16[8,24,17,272]{3,2,1,0:T(8,128)(2,1)S(1)} %copy.111) | data formatting | bytes 3551232 | tf_op jit(solution)/shard_map/reshape | solution.py:632
  59.3 1.9 fusion.36
  61.3 1.2 pad.82
  62.5 1.2 pad.83
  63.8 0.7 broadcast_in_dim.45.coli
  64.4 51.4 %regress.1 = (bf16[1024,4864]{1,0:T(8,128)(2,1)}, f32[128,4864]{1,0:T(8,128)}, f32[128,128]{1,0:T(8,128)}, f32[48,128]{1,0:T(8,128)}, bf16[48,928,128]{2,1,0:T(8,128)(2,1)}) custom-call(s32[5]{0:T(128)} %stack.54.meta, s32[48]{0:T(128)} %select_reduce_fusion.order, s32[48]{0:T(128)} %broadcast_select_fusion.1.tab_r, s32[48]{0:T(128)} %copy-done.18, ...), custom_call_target="tpu_custom_call" | custom-call | tf_op jit(solution)/shard_map/regress/pallas_call | solution.py:476
  115.9 10.8 %pool.1.lift = f32[48,128]{1,0:T(8,128)} custom-call(f32[128,128]{1,0:T(8,128)} %get-tuple-element.9.part, f32[48,128]{1,0:T(8,128)} %get-tuple-element.10.ring, f32[128,128]{1,0:T(8,128)} %convert_element_type.63.pool), custom_call_target="tpu_custom_call" | custom-call | tf_op jit(solution)/shard_map/pool/pallas_call | solution.py:597
  126.7 65.5 %patches.1 = f32[128,4864]{1,0:T(8,128)} custom-call(s32[5]{0:T(128)} %stack.54.meta, s32[48]{0:T(128)} %select_reduce_fusion.order, s32[48]{0:T(128)} %broadcast_select_fusion.1.tab_r, s32[48]{0:T(128)} %copy-done.18, bf16[1024,4864]{1,0:T(8,128)(2,1)} %get-tuple-element.7.first, bf16[48,928,128]{2,1,0:T(8,128)(2,1)} %get-tuple-element.8.strips, ...), custom_call_target="tpu_custom_call" | custom-call | tf_op jit(solution)/shard_map/patches/pallas_call | solution.py:504
  192.3 1.8 slice.123
  194.1 3.1 %reshape.314 = f32[8,16,17,272]{3,2,1,0:T(8,128)} reshape(f32[8,16,4624]{2,1,0:T(8,128)S(1)} %slice.123) | data formatting | bytes 4734976 | tf_op jit(solution)/shard_map/reshape | solution.py:720
  197.2 6.1 %copy.140 = f32[16,17,8,272]{3,2,1,0:T(8,128)} copy(f32[16,17,8,272]{3,1,0,2:T(8,128)} %bitcast.101) | data formatting | bytes 4734976 | tf_op jit(solution)/shard_map/transpose | solution.py:721
  203.5 3.1 %reshape.317 = f32[8,16,17,272]{3,2,1,0:T(8,128)} reshape(f32[8,16,4624]{2,1,0:T(8,128)S(1)} %slice.125) | data formatting | bytes 4734976 | tf_op jit(solution)/shard_map/reshape | solution.py:720
  206.6 4.4 %copy.139 = f32[16,17,8,272]{3,2,1,0:T(8,128)S(1)} copy(f32[16,17,8,272]{3,1,0,2:T(8,128)} %bitcast.102) | data formatting | bytes 4734976 | tf_op jit(solution)/shard_map/transpose | solution.py:721
  211.0 4.7 %slice_add_fusion = (f32[12,128,256]{2,1,0:T(8,128)}, f32[12,128,256]{2,1,0:T(8,128)}) fusion(f32[16,136,272]{2,1,0:T(8,128)S(1)} %bitcast.105, f32[16,136,272]{2,1,0:T(8,128)} %bitcast.104, f32[12,128,256]{2,1,0:T(8,128)S(1)} %copy-done.1, f32[]{:T(128)} %bitcast.1, f32[]{:T(128)} %bitcast), kind=kLoop, calls=%fused_computation.16 | loop fusion | flops 2752512 | bytes 7864328 | tf_op jit(solution)/shard_map/add | solution.py:728
  (83 shorter events, 2.0 us)
Async XLA Ops:
  0.6 16.2 %copy-start.20 = (s32[1,16,2]{1,2,0:T(2,128)S(1)}, s32[1,16,2]{1,2,0:T(2,128)}, u32[]{:S(2)}) copy-start(s32[1,16,2]{1,2,0:T(2,128)} %param.21) | copy-start | bytes 388
  0.6 9.1 %copy-start = (bf16[12,128,256]{2,1,0:T(8,128)(2,1)S(1)}, bf16[12,128,256]{2,1,0:T(8,128)(2,1)}, u32[]{:S(2)}) copy-start(bf16[12,128,256]{2,1,0:T(8,128)(2,1)} %param.12) | copy-start | bytes 2359300
  0.7 15.4 %copy-start.14 = (bf16[9,128,24]{1,2,0:T(8,128)(2,1)S(1)}, bf16[9,128,24]{1,2,0:T(8,128)(2,1)}, u32[]{:S(2)}) copy-start(bf16[9,128,24]{1,2,0:T(8,128)(2,1)} %param.17) | copy-start | bytes 165892
  2.7 31.6 %collective-permute-start.1 = (s32[17,2]{0,1:T(2,128)}, s32[17,2]{0,1:T(2,128)}, u32[]{:S(2)}, u32[]{:S(2)}) collective-permute-start(s32[17,2]{0,1:T(2,128)} %concatenate.24), channel_id=1, source_target_pairs={{16,0},{32,16},{48,32},{64,48},{80,64},{96,80},{112,96},{17,1},{33... | collective-permute-start | bytes 416 | tf_op jit(solution)/shard_map/ppermute | solution.py:445
  4.8 29.4 %collective-permute-start = (s32[17,2]{0,1:T(2,128)}, s32[17,2]{0,1:T(2,128)}, u32[]{:S(2)}, u32[]{:S(2)}) collective-permute-start(s32[17,2]{0,1:T(2,128)} %concatenate.24), channel_id=1, source_target_pairs={{0,16},{16,32},{32,48},{48,64},{64,80},{80,96},{96,112},{1,17},{17... | collective-permute-start | bytes 416 | tf_op jit(solution)/shard_map/ppermute | solution.py:445
  9.8 14.4 %copy-start.15 = (bf16[9,128,12]{1,2,0:T(8,128)(2,1)S(1)}, bf16[9,128,12]{1,2,0:T(8,128)(2,1)}, u32[]{:S(2)}) copy-start(bf16[9,128,12]{1,2,0:T(8,128)(2,1)} %param.15) | copy-start | bytes 82948
  9.8 15.9 %copy-start.16 = (bf16[9,12,128]{2,1,0:T(8,128)(2,1)S(1)}, bf16[9,12,128]{2,1,0:T(8,128)(2,1)}, u32[]{:S(2)}) copy-start(bf16[9,12,128]{2,1,0:T(8,128)(2,1)} %param.16) | copy-start | bytes 82948
  9.8 16.6 %copy-start.17 = (bf16[128,128]{1,0:T(8,128)(2,1)S(1)}, bf16[128,128]{1,0:T(8,128)(2,1)}, u32[]{:S(2)}) copy-start(bf16[128,128]{1,0:T(8,128)(2,1)} %param.19) | copy-start | bytes 98308
  10.5 28.0 %collective-permute-start.2 = (bf16[24,4,256]{2,1,0:T(4,128)(2,1)}, bf16[24,4,256]{2,1,0:T(4,128)(2,1)S(1)}, u32[]{:S(2)}, u32[]{:S(2)}) collective-permute-start(bf16[24,4,256]{2,1,0:T(4,128)(2,1)} %get-tuple-element.30), channel_id=1, source_target_pairs={{0,16},{16,32},{32,48},{48,64},{64,80},{80,96},{96,112},{1,17},{17... | collective-permute-start | bytes 147464 | tf_op jit(solution)/shard_map/ppermute | solution.py:445
  12.4 26.1 %collective-permute-start.3 = (bf16[24,4,256]{2,1,0:T(4,128)(2,1)}, bf16[24,4,256]{2,1,0:T(4,128)(2,1)S(1)}, u32[]{:S(2)}, u32[]{:S(2)}) collective-permute-start(bf16[24,4,256]{2,1,0:T(4,128)(2,1)} %get-tuple-element.31), channel_id=1, source_target_pairs={{16,0},{32,16},{48,32},{64,48},{80,64},{96,80},{112,96},{17,1},{33... | collective-permute-start | bytes 147464 | tf_op jit(solution)/shard_map/ppermute | solution.py:445
  23.9 2.5 %copy-start.3 = (bf16[9,32,128]{2,1,0:T(8,128)(2,1)}, bf16[9,32,128]{2,1,0:T(8,128)(2,1)S(1)}, u32[]{:S(2)}) copy-start(bf16[9,32,128]{2,1,0:T(8,128)(2,1)S(1)} %pad.92.wcol) | copy-start | bytes 221188
  28.3 5.1 %copy-start.4 = (bf16[128,8]{1,0:T(8,128)(2,1)S(1)}, bf16[128,8]{1,0:T(8,128)(2,1)}, u32[]{:S(2)}) copy-start(bf16[128,8]{1,0:T(8,128)(2,1)} %copy.115) | copy-start | bytes 6148
  28.3 5.0 %copy-start.5 = (bf16[128,8]{1,0:T(8,128)(2,1)S(1)}, bf16[128,8]{1,0:T(8,128)(2,1)}, u32[]{:S(2)}) copy-start(bf16[128,8]{1,0:T(8,128)(2,1)} %copy.116) | copy-start | bytes 6148
  28.3 5.0 %copy-start.6 = (bf16[128,8]{1,0:T(8,128)(2,1)S(1)}, bf16[128,8]{1,0:T(8,128)(2,1)}, u32[]{:S(2)}) copy-start(bf16[128,8]{1,0:T(8,128)(2,1)} %copy.117) | copy-start | bytes 6148
  28.4 5.0 %copy-start.7 = (bf16[128,8]{1,0:T(8,128)(2,1)S(1)}, bf16[128,8]{1,0:T(8,128)(2,1)}, u32[]{:S(2)}) copy-start(bf16[128,8]{1,0:T(8,128)(2,1)} %copy.118) | copy-start | bytes 6148
  28.4 5.0 %copy-start.8 = (bf16[128,8]{1,0:T(8,128)(2,1)S(1)}, bf16[128,8]{1,0:T(8,128)(2,1)}, u32[]{:S(2)}) copy-start(bf16[128,8]{1,0:T(8,128)(2,1)} %copy.119) | copy-start | bytes 6148
  28.4 5.0 %copy-start.9 = (bf16[128,8]{1,0:T(8,128)(2,1)S(1)}, bf16[128,8]{1,0:T(8,128)(2,1)}, u32[]{:S(2)}) copy-start(bf16[128,8]{1,0:T(8,128)(2,1)} %copy.120) | copy-start | bytes 6148
  28.4 5.0 %copy-start.10 = (bf16[128,8]{1,0:T(8,128)(2,1)S(1)}, bf16[128,8]{1,0:T(8,128)(2,1)}, u32[]{:S(2)}) copy-start(bf16[128,8]{1,0:T(8,128)(2,1)} %copy.121) | copy-start | bytes 6148
  28.4 5.0 %copy-start.11 = (bf16[128,8]{1,0:T(8,128)(2,1)S(1)}, bf16[128,8]{1,0:T(8,128)(2,1)}, u32[]{:S(2)}) copy-start(bf16[128,8]{1,0:T(8,128)(2,1)} %copy.122) | copy-start | bytes 6148
  28.4 5.0 %copy-start.12 = (bf16[128,8]{1,0:T(8,128)(2,1)S(1)}, bf16[128,8]{1,0:T(8,128)(2,1)}, u32[]{:S(2)}) copy-start(bf16[128,8]{1,0:T(8,128)(2,1)} %copy.123) | copy-start | bytes 6148
  28.4 5.9 %copy-start.21 = (s32[1,17,2]{1,2,0:T(2,128)S(1)}, s32[1,17,2]{1,2,0:T(2,128)}, u32[]{:S(2)}) copy-start(s32[1,17,2]{1,2,0:T(2,128)} %pad_bitcast_fusion.8) | copy-start | bytes 412
  36.0 11.0 %copy-start.18 = (s32[48]{0:T(128)}, s32[48]{0:T(128)S(1)}, u32[]{:S(2)}) copy-start(s32[48]{0:T(128)S(1)} %get-tuple-element.14.tab_c) | copy-start | bytes 580
  39.5 7.5 %copy-start.19 = (s32[48]{0:T(128)S(1)}, s32[48]{0:T(128)}, u32[]{:S(2)}) copy-start(s32[48]{0:T(128)} %broadcast_select_fusion.1.tab_r) | copy-start | bytes 580
  40.5 8.5 %collective-permute-start.4 = (bf16[24,136,4]{1,0,2:T(8,128)(2,1)S(1)}, bf16[24,136,4]{1,0,2:T(8,128)(2,1)S(1)}, u32[]{:S(2)}, u32[]{:S(2)}) collective-permute-start(bf16[24,136,4]{1,0,2:T(8,128)(2,1)S(1)} %copy.107), channel_id=1, source_target_pairs={{0,1},{1,2},{2,3},{3,4},{4,5},{5,6},{6,7},{7,8},{8,9},{9,10},{10,1... | collective-permute-start | bytes 78344 | tf_op jit(solution)/shard_map/ppermute | solution.py:445
  44.2 6.0 %collective-permute-start.5 = (bf16[24,136,4]{1,0,2:T(8,128)(2,1)S(1)}, bf16[24,136,4]{1,0,2:T(8,128)(2,1)S(1)}, u32[]{:S(2)}, u32[]{:S(2)}) collective-permute-start(bf16[24,136,4]{1,0,2:T(8,128)(2,1)S(1)} %copy.108), channel_id=1, source_target_pairs={{1,0},{2,1},{3,2},{4,3},{5,4},{6,5},{7,6},{8,7},{9,8},{10,9},{11,1... | collective-permute-start | bytes 78344 | tf_op jit(solution)/shard_map/ppermute | solution.py:445
  61.3 2.5 %copy-start.13 = (s32[4864]{0:T(1024)S(1)}, s32[4864]{0:T(1024)}, u32[]{:S(2)}) copy-start(s32[4864]{0:T(1024)} %fusion.22) | copy-start | bytes 58372
  197.2 6.1 %copy-start.2 = (f32[128,4864]{1,0:T(8,128)S(1)}, f32[128,4864]{1,0:T(8,128)}, u32[]{:S(2)}) copy-start(f32[128,4864]{1,0:T(8,128)} %get-tuple-element.11) | copy-start | bytes 7471108
  206.6 4.4 %copy-start.1 = (f32[12,128,256]{2,1,0:T(8,128)S(1)}, f32[12,128,256]{2,1,0:T(8,128)}, u32[]{:S(2)}) copy-start(f32[12,128,256]{2,1,0:T(8,128)} %param.13) | copy-start | bytes 4718596

commit v3 on v2

--- a/solution.py
+++ b/solution.py
@@ -2,6 +2,7 @@
 
 import jax
 import jax.numpy as jnp
+import numpy as np
 from jax import lax
 from jax.experimental import pallas as pl
 from jax.experimental.pallas import tpu as pltpu
@@ -11,10 +12,12 @@
 step_ratio = 0.6
 
 HALO = 4
-STRIDE = 272
+TOP = 8
+STRIDE = 264
+STRIP = 272
 PLANES = 8
 PAD = 384
-FRONT = 544
+FRONT = 528
 STEP = 256
 TILE = 512
 COLUMN = 24
@@ -75,18 +78,59 @@
     return planes
 
 
+def gather_pair(raw, out):
+    zero = jnp.zeros((128, 16 - raw.shape[2]), bf16)
+    parts = []
+    for t in range(9):
+        parts += [raw[t] * 0.5, zero]
+    gap = jnp.zeros((128, 48), bf16)
+    out[:128, :] = jnp.concatenate(parts + [gap], 1)
+    out[128:, :] = jnp.concatenate([gap] + parts, 1)
+
+
+def spread_pair(raw, out, front):
+    zeros = [jnp.zeros((n, 128), f32) for n in (front, 16 - front - raw.shape[1]) if n]
+    parts = []
+    for a in (2, 1, 0):
+        for b in range(3):
+            taps = raw[3 * a + b].astype(f32)
+            parts += [zeros[0], taps] if front else [taps, zeros[0]]
+    gap = jnp.zeros((48, 128), f32)
+    out[:, :128] = jnp.concatenate(parts + [gap], 0).astype(bf16)
+    out[:, 128:] = jnp.concatenate([gap] + parts, 0).astype(bf16)
+
+
 def regress_kernel(
     rows, patch, tile_r, tile_c,
-    meta, order, tab_r, tab_c,
-    coarse, latent, rowi, coli, r0v, c0v, w1, w2, w3, wrow, wcol,
-    first_out, mean_out, part_out, ring_out, strips_out,
-    sums, cond_a, cond_b, cond_c, sbuf, sem,
+    meta, tabs, coarse, latent, rowi, coli, tabs_v, raw1, raw2, raw3,
+    first_out, mean_out, part_out, ring_out, strips_out, order,
+    w1, w2, w3, sums, cond_a, cond_b, cond_c, sbuf, sem,
 ):
     size = lanes_of(rows)
     steps = size // STEP
     cells = size + 2 * FRONT
     groups = rows // PLANES
-    row_lo, row_hi, col_lo, col_hi, number = (meta[0], meta[1], meta[2], meta[3], meta[4])
+    row_lo, row_hi, col_lo, col_hi = meta[0], meta[1], meta[2], meta[3]
+    gather_pair(raw1, w1)
+    spread_pair(raw2, w2, 4)
+    zero8 = jnp.zeros((128, 8), bf16)
+    w3[...] = 0.5 * jnp.concatenate(
+        [raw3[t][:, :16] for t in range(9)]
+        + [raw3[t][:, 16:] for t in (0, 1, 3, 4, 6, 7, 2, 5, 8)] + [zero8], 1
+    )
+
+    def enlist(q, n):
+        live = tabs[0, q] < FAR
+
+        @pl.when(live)
+        def _():
+            order[n] = q
+
+        return n + live.astype(jnp.int32)
+
+    entries = ring_out.shape[0]
+    number = lax.fori_loop(0, entries, enlist, jnp.int32(0))
+    order[entries] = number
     for ref in (sums, cond_a, cond_b):
         ref[:, :PAD] = jnp.zeros((ref.shape[0], PAD), ref.dtype)
         ref[:, PAD + size :] = jnp.zeros((ref.shape[0], PAD), ref.dtype)
@@ -161,7 +205,7 @@
         split = (group + 1) * STRIDE - base
         later = lane >= split
         col = lane + base - group * STRIDE - jnp.where(later, STRIDE, 0)
-        c0b, r0b = c0v[...], r0v[...]
+        r0b, c0b = tabs_v[:1], tabs_v[1:2]
         wanted = (
             (col > c0b) & (col < c0b + (patch - 1)) & (col >= HALO) & (col < HALO + tile_c)
         )
@@ -170,7 +214,7 @@
 
         def row_keep(row):
             keep = (
-                (r0b < row) & (row < r0b + (patch - 1)) & (row >= HALO) & (row < HALO + tile_r)
+                (r0b < row) & (row < r0b + (patch - 1)) & (row >= TOP) & (row < TOP + tile_r)
             )
             return jnp.where(keep, 1.0, 0.0).astype(bf16)
 
@@ -199,7 +243,7 @@
     @pl.loop(0, number)
     def _(n):
         q = order[n]
-        r0, c0 = tab_r[q], tab_c[q]
+        r0, c0 = tabs[0, q], tabs[1, q]
         r1, c1 = r0 + patch - 1, c0 + patch - 1
 
         def add(value, weight):
@@ -208,7 +252,7 @@
 
         for s, (r, height) in enumerate(((r0, (1, 2)), (r1, (0, 1)))):
 
-            @pl.when((r >= HALO - 1) & (r <= HALO + tile_r))
+            @pl.when((r >= TOP - 1) & (r <= TOP + tile_r))
             def _(s=s, r=r, height=height):
                 total = None
                 for a in height:
@@ -218,13 +262,16 @@
                     for b in range(3):
                         x = cond_c[pl.ds(start + b - 1, STRIDE), :]
                         x = jnp.where((j + (b - 1) >= c0) & (j + (b - 1) <= c1), x, 0.0)
-                        term = jnp.dot(
-                            x.astype(bf16), wrow[plane % 4, 3 * a + b], preferred_element_type=f32
+                        x = pltpu.roll(x, (128 - plane % 4 * 32) % 128, 1)[:, :24].astype(bf16)
+                        term = lax.dot_general(
+                            x, raw3[3 * a + b], (((1,), (1,)), ((), ())), preferred_element_type=f32
                         )
                         total = term if total is None else total + term
-                value = silu_half(total).astype(bf16)
-                sbuf[STRIDE * s : STRIDE * s + STRIDE, :] = value
-                own = (r >= HALO) & (r < HALO + tile_r)
+                value = silu_half(0.5 * total)
+                tail = jnp.zeros((STRIP - STRIDE, 128), f32)
+                sbuf[STRIP * s : STRIP * s + STRIP, :] = jnp.concatenate([value, tail], 0).astype(bf16)
+                value = value.astype(bf16)
+                own = (r >= TOP) & (r < TOP + tile_r)
                 add(value, own & (j >= c0) & (j <= c1) & (j >= HALO) & (j < HALO + tile_c))
 
         for s, (c, breadth) in enumerate(((c0, (1, 2)), (c1, (0, 1)))):
@@ -247,14 +294,16 @@
                     for a in range(3):
                         x = jnp.concatenate(planes[a : a + PLANES], 0)
                         inside = (i + (a - 1) >= r0) & (i + (a - 1) <= r1)
-                        x = jnp.where(inside[:, :32], x, 0.0).astype(bf16)
-                        term = jnp.dot(x, wcol[3 * a + b], preferred_element_type=f32)
+                        x = jnp.where(inside[:, :32], x, 0.0)[:, :24].astype(bf16)
+                        term = lax.dot_general(
+                            x, raw3[3 * a + b], (((1,), (1,)), ((), ())), preferred_element_type=f32
+                        )
                         total = term if total is None else total + term
-                value = silu_half(total).astype(bf16)
-                lo = 2 * STRIDE + PLANES * COLUMN * s
+                value = silu_half(0.5 * total).astype(bf16)
+                lo = 2 * STRIP + PLANES * COLUMN * s
                 sbuf[lo : lo + PLANES * COLUMN, :] = value
                 own = (c >= HALO) & (c < HALO + tile_c) & live
-                add(value, own & (i > r0) & (i < r1) & (i >= HALO) & (i < HALO + tile_r))
+                add(value, own & (i > r0) & (i < r1) & (i >= TOP) & (i < TOP + tile_r))
 
         copy = pltpu.make_async_copy(sbuf, strips_out.at[n], sem)
         copy.start()
@@ -263,16 +312,21 @@
 
 def patch_kernel(
     rows, patch, tile_r, tile_c,
-    meta, order, tab_r, tab_c,
-    first, strips, lift, weight, w4, w5,
-    out,
-    m, acc, sbuf, keep_row, keep_col, wbuf, sem,
+    order, tabs, noise, first, strips, lift, weight, mean, latent, middle, raw5,
+    next_out, est_out,
+    w5, m, acc, sbuf, keep_row, keep_col, wbuf, sem,
 ):
     size = lanes_of(rows)
     steps = size // STEP
     groups = rows // PLANES
-    number = meta[4]
-    high = 2 * STRIDE
+    number = order[lift.shape[0]]
+    spread_pair(raw5, w5, 0)
+
+    def mixed(x, dim):
+        return 0.5 * lax.dot_general(
+            x, middle[...], (((dim,), (1,)), ((), ())), preferred_element_type=f32
+        )
+    high = 2 * STRIP
     tall = PLANES * COLUMN
 
     def fetch(n):
@@ -287,8 +341,7 @@
         base = pl.multiple_of(k * STEP, 128)
         for i in range(PLANES):
             x = first[128 * i : 128 * i + 128, pl.ds(base, STEP)]
-            y = lax.dot_general(x, w4[...], (((0,), (0,)), ((), ())), preferred_element_type=f32)
-            m[pl.ds(base + i * size, STEP), :] = y
+            m[pl.ds(base + i * size, STEP), :] = mixed(x, 0)
 
     acc[...] = jnp.zeros_like(acc)
     m[PLANES * size :, :] = jnp.zeros((TILE, 128), f32)
@@ -300,7 +353,7 @@
     @pl.loop(0, number)
     def _(n):
         q = order[n]
-        r0, c0 = tab_r[q], tab_c[q]
+        r0, c0 = tabs[0, q], tabs[1, q]
         r1, c1 = r0 + patch - 1, c0 + patch - 1
         slot = n % 2
         fetch(n).wait()
@@ -312,7 +365,7 @@
         half_lift = lift[pl.ds(q, 1), :]
 
         def row_ok(r):
-            return (r >= HALO - 1) & (r <= HALO + tile_r)
+            return (r >= TOP - 1) & (r <= TOP + tile_r)
 
         def col_ok(c):
             return (c >= HALO - 1) & (c <= HALO + tile_c)
@@ -331,7 +384,7 @@
             def _(s=s, c=c, source=source):
                 if source is not None:
                     strip = sbuf[slot, high + tall * source : high + tall * source + tall, :]
-                    got = jnp.dot(strip, w4[...], preferred_element_type=f32)
+                    got = mixed(strip, 1)
                 for i in range(PLANES):
                     keep_col[s, i, :groups, :] = m[col_at(c, i), :]
                     if source is None:
@@ -350,8 +403,8 @@
                 if source is None:
                     m[row_at(r), :] = jnp.full((STRIDE, 128), NEG, f32)
                 else:
-                    strip = sbuf[slot, STRIDE * source : STRIDE * source + STRIDE, :]
-                    got = jnp.dot(strip, w4[...], preferred_element_type=f32)
+                    strip = sbuf[slot, STRIP * source : STRIP * source + STRIP, :]
+                    got = mixed(strip, 1)[:STRIDE]
                     m[row_at(r), :] = jnp.where((j >= c0) & (j <= c1), got, NEG)
 
         top = r0 // PLANES
@@ -359,8 +412,8 @@
         move = top * STRIDE + c0
         shifts = (move, move + STRIDE, jnp.where(phase == 0, move - STRIDE, move))
         clo, chi = jnp.maximum(c0, HALO - 1), jnp.minimum(c1, HALO + tile_c)
-        glo = jnp.maximum(r0, HALO - 1) // PLANES
-        ghi = jnp.minimum(r1, HALO + tile_r) // PLANES
+        glo = jnp.maximum(r0, TOP - 1) // PLANES
+        ghi = jnp.minimum(r1, TOP + tile_r) // PLANES
 
         @pl.loop((glo * STRIDE + clo) // TILE, (ghi * STRIDE + chi) // TILE + 1)
         def _(k):
@@ -429,36 +482,33 @@
                 for i in range(PLANES):
                     m[col_at(c, i), :] = keep_col[s, i, :groups, :]
 
-    @pl.loop(0, steps)
-    def _(k):
-        base = pl.multiple_of(k * STEP, 128)
-        planes = combined(acc, base, STEP)
-        out[:, pl.ds(base, STEP)] = jnp.concatenate([p / (1.0 + p[12:13]) for p in planes], 0)
-
-
+    for k in range(tile_r // PLANES):
+        start = (k + TOP // PLANES) * STRIDE + HALO
+        whole = start // 128 * 128
+        off = start - whole
+        span = -(-(off + tile_c) // 128) * 128
+        planes = combined(acc, whole, span)
+        got = jnp.stack([p / (1.0 + p[12:13]) for p in planes], 0)[:, :, off : off + tile_c]
+        got = jnp.swapaxes(got, 0, 1)[:12]
+        base = mean[:, whole : whole + span].reshape(PLANES, 16, span)[:, :, off : off + tile_c]
+        base = jnp.swapaxes(base, 0, 1)[4:]
+        rows_at = slice(PLANES * k, PLANES * k + PLANES)
+        scale_in, skip, scale_out = precondition(noise)
+        lat = latent[:, rows_at, :]
+        denoised = skip * lat + scale_out * got
+        next_out[:, rows_at, :] = lat + (step_ratio - 1.0) * (lat - denoised)
+        est_out[:, rows_at, :] = base + denoised
+
+
+FAR = 1 << 20
 WFRONT = 2048
 
 
-def passed(block, axis, step):
-    count = lax.axis_size(axis)
-    route = [(i, i + step) for i in range(count) if 0 <= i + step < count]
-    return lax.ppermute(block, axis, route)
-
-
-def with_halo(cells, axis, dim, width):
-    head = lax.slice_in_dim(cells, 0, width, axis=dim)
-    tail = lax.slice_in_dim(cells, cells.shape[dim] - width, cells.shape[dim], axis=dim)
-    return jnp.concatenate([passed(tail, axis, 1), cells, passed(head, axis, -1)], axis=dim)
-
-
-def precondition(noise_level):
-    level = noise_level[0]
+def precondition(noise):
+    level = jnp.full((1, 1, 1), noise[0], f32)
     spread = level * level + sigma_data * sigma_data
-    return (
-        1.0 / jnp.sqrt(spread),
-        sigma_data * sigma_data / spread,
-        level * sigma_data / jnp.sqrt(spread),
-    )
+    root = jnp.sqrt(spread)
+    return 1.0 / root, sigma_data * sigma_data / spread, level * sigma_data / root
 
 
 def specs():
@@ -475,21 +525,25 @@
     cells = size + 2 * FRONT
     return pl.pallas_call(
         functools.partial(regress_kernel, *fixed),
-        in_specs=[smem] * 4 + [vmem] * 11,
-        out_specs=[vmem, vmem, vmem, vmem, anyw],
+        in_specs=[smem] * 2 + [vmem] * 8,
+        out_specs=[vmem, vmem, vmem, vmem, anyw, smem],
         out_shape=[
             jax.ShapeDtypeStruct((PLANES * 128, size), bf16),
             jax.ShapeDtypeStruct((PLANES * 16, size), f32),
             jax.ShapeDtypeStruct((128, 128), f32),
             jax.ShapeDtypeStruct((entries, 128), f32),
-            jax.ShapeDtypeStruct((entries, 2 * (STRIDE + PLANES * COLUMN), 128), bf16),
+            jax.ShapeDtypeStruct((entries, 2 * (STRIP + PLANES * COLUMN), 128), bf16),
+            jax.ShapeDtypeStruct((entries + 1,), jnp.int32),
         ],
         scratch_shapes=[
+            pltpu.VMEM((256, 192), bf16),
+            pltpu.VMEM((192, 256), bf16),
+            pltpu.VMEM((128, 224), bf16),
             pltpu.VMEM((48 * (PLANES + 2), size + 2 * PAD), f32),
             pltpu.VMEM((16 * PLANES, size + 2 * PAD), bf16),
             pltpu.VMEM((8 * PLANES, size + 2 * PAD), f32),
             pltpu.VMEM((2 * cells + COLUMN * STRIDE - size + STRIDE, 128), f32),
-            pltpu.VMEM((2 * (STRIDE + PLANES * COLUMN), 128), bf16),
+            pltpu.VMEM((2 * (STRIP + PLANES * COLUMN), 128), bf16),
             pltpu.SemaphoreType.DMA,
         ],
         compiler_params=pltpu.CompilerParams(vmem_limit_bytes=VMEM),
@@ -503,13 +557,14 @@
     smem, vmem, anyw = specs()
     return pl.pallas_call(
         functools.partial(patch_kernel, *fixed),
-        in_specs=[smem] * 4 + [vmem, anyw] + [vmem] * 4,
-        out_specs=vmem,
-        out_shape=jax.ShapeDtypeStruct((PLANES * 16, size), f32),
+        in_specs=[smem] * 3 + [vmem, anyw] + [vmem] * 6,
+        out_specs=[vmem] * 2,
+        out_shape=[jax.ShapeDtypeStruct((12, fixed[2], fixed[3]), f32)] * 2,
         scratch_shapes=[
+            pltpu.VMEM((192, 256), bf16),
             pltpu.VMEM((PLANES * size + TILE, 128), f32),
             pltpu.VMEM((48 * (PLANES + 2), size + 2 * PAD), f32),
-            pltpu.VMEM((2, 2 * (STRIDE + PLANES * COLUMN), 128), bf16),
+            pltpu.VMEM((2, 2 * (STRIP + PLANES * COLUMN), 128), bf16),
             pltpu.VMEM((4, STRIDE, 128), f32),
             pltpu.VMEM((4, PLANES, COLUMN, 128), f32),
             pltpu.VMEM((72, TILE), f32),
@@ -586,9 +641,164 @@
             copies[x].wait_send()
 
     lift[...] = 0.5 * lax.dot_general(
-        lift[...] / cells, pool[...], (((1,), (1,)), ((), ())),
+        lift[...] / cells, pool[...].astype(f32), (((1,), (1,)), ((), ())),
         precision=lax.Precision.HIGHEST, preferred_element_type=f32,
     )
+
+
+SIDES = [(-1, 0), (1, 0), (0, -1), (0, 1), (-1, -1), (-1, 1), (1, -1), (1, 1)]
+
+
+def frame_kernel(
+    shape, per_slab, patch,
+    noise, coarse, latent, table, move, ends, back,
+    coarse_out, latent_out, tabs_out,
+    both, framed, edge_rows, edge_cols, corners, strip, tables, send, recv,
+):
+    channels, tile_r, tile_c = latent.shape
+    around = neighbours(SIDES, shape)
+    there = [a[0] for a in around]
+    scale_in = precondition(noise)[0]
+    both[:channels, :, :] = coarse[...]
+    both[channels:, :, :] = (scale_in * latent[...]).astype(bf16)
+    greet(around)
+
+    def last(d):
+        return slice(0, 16) if d < 0 else slice(tile_r - 16, tile_r)
+
+    def side(d):
+        return slice(0, 128) if d < 0 else slice(tile_c - 128, tile_c)
+
+    opposite = [SIDES.index((-a, -b)) for a, b in SIDES]
+    copies = []
+
+    def copy(x, source, target, slot):
+        here = opposite[x]
+        return pltpu.make_async_remote_copy(
+            src_ref=source, dst_ref=target, send_sem=send.at[slot, x], recv_sem=recv.at[slot, here],
+            device_id=around[x][1], device_id_type=MESH,
+        )
+
+    def begin(x, one):
+        copies.append((x, one))
+
+        @pl.when(there[x])
+        def _():
+            one.start()
+
+    for x in (0, 1):
+        begin(x, copy(x, both.at[:, last(SIDES[x][0]), :], edge_rows.at[opposite[x]], 0))
+        begin(x, copy(x, table, tables.at[opposite[x]], 1))
+    for x in range(4, 8):
+        di, dj = SIDES[x]
+        begin(x, copy(x, both.at[:, last(di), side(dj)], corners.at[opposite[x] - 4], 0))
+    flat = both[...].reshape(2 * channels * tile_r, tile_c)
+    strip[...] = lax.dot_general(
+        ends[...], flat, (((1,), (1,)), ((), ())), preferred_element_type=f32
+    )
+    for x in (2, 3):
+        begin(x, copy(x, strip, edge_cols.at[opposite[x] - 2], 0))
+
+    @pl.loop(0, 2 * channels)
+    def _(c):
+        x = jnp.dot(both[c], move[...], preferred_element_type=f32)
+        framed[c + c // channels * (16 - channels), TOP : TOP + tile_r, :] = x
+
+    for x in range(8):
+
+        @pl.when(jnp.logical_not(there[x]))
+        def _(x=x):
+            if x < 2:
+                edge_rows[x] = jnp.zeros(edge_rows.shape[1:], bf16)
+                tables[x] = jnp.zeros(tables.shape[1:], jnp.int32)
+            elif x < 4:
+                edge_cols[x - 2] = jnp.zeros(edge_cols.shape[1:], f32)
+            else:
+                corners[x - 4] = jnp.zeros(corners.shape[1:], bf16)
+
+    for x, one in copies:
+
+        @pl.when(there[x])
+        def _(one=one):
+            one.wait_send()
+
+    for x, one in copies:
+
+        @pl.when(there[opposite[x]])
+        def _(one=one):
+            one.wait_recv()
+
+    for c in range(2 * channels):
+        at = c + c // channels * (16 - channels)
+        cols = jnp.concatenate(
+            [edge_cols[x][:, tile_r * c : tile_r * c + tile_r] for x in range(2)], 0
+        ).astype(bf16)
+        framed[at, TOP : TOP + tile_r, :] += lax.dot_general(
+            cols, back[256:272, :], (((0,), (0,)), ((), ())), preferred_element_type=f32
+        )
+        for x, rows_at in ((0, slice(0, TOP)), (1, slice(TOP + tile_r, 2 * TOP + tile_r))):
+            x4 = 4 + 2 * x
+            got = jnp.dot(edge_rows[x, c], move[...], preferred_element_type=f32)
+            got += jnp.dot(corners[x4 - 4, c], back[:128, :], preferred_element_type=f32)
+            got += jnp.dot(corners[x4 - 3, c], back[128:256, :], preferred_element_type=f32)
+            framed[at, rows_at, :] = got[16 - TOP :] if x == 0 else got[:TOP]
+    zero = jnp.zeros((16 - channels, tile_r + 2 * TOP, STRIDE), f32)
+    framed[channels:16] = zero
+    framed[16 + channels :] = zero
+    groups = (tile_r + 2 * TOP) // PLANES
+    parts = []
+    for g in range(groups):
+        block = framed[:, PLANES * g : PLANES * g + PLANES, :]
+        parts.append(jnp.swapaxes(block, 0, 1))
+    rest = coarse_out.shape[1] - PAD - groups * STRIDE
+    for i in range(PLANES):
+        row = jnp.concatenate(
+            [jnp.zeros((32, PAD), f32)] + [p[i] for p in parts] + [jnp.zeros((32, rest), f32)], 1
+        ).astype(bf16)
+        coarse_out[16 * i : 16 * i + 16, :] = row[:16]
+        latent_out[16 * i : 16 * i + 16, :] = row[16:]
+
+    lane = lax.broadcasted_iota(jnp.int32, (8, 128), 1)
+    got = jnp.where(lane < per_slab, tables[0], jnp.where(lane < 2 * per_slab, table[...], tables[1]))
+    row0 = got[:1] - (lax.axis_index("slab") * tile_r - TOP)
+    col0 = got[1:2] - (lax.axis_index("patch") * tile_c - HALO)
+    live = (got[3:4] < got[2:3]) & (lane[:1] < 3 * per_slab)
+    live = live & (row0 < TOP + tile_r) & (row0 + patch > TOP)
+    live = live & (col0 < HALO + tile_c) & (col0 + patch > HALO)
+    tabs_out[...] = jnp.concatenate(
+        [jnp.where(live, row0, FAR), jnp.where(live, col0, FAR), lane[:6]], 0
+    )
+
+
+def run_frame(shape, per_slab, patch, tile, *args):
+    channels, tile_r, tile_c = tile
+    smem, vmem, anyw = specs()
+    lanes = lanes_of(tile_r + 2 * TOP) + 2 * PAD
+    return pl.pallas_call(
+        functools.partial(frame_kernel, shape, per_slab, patch),
+        in_specs=[smem] + [vmem] * 6,
+        out_specs=[vmem] * 3,
+        out_shape=[
+            jax.ShapeDtypeStruct((PLANES * 16, lanes), bf16),
+            jax.ShapeDtypeStruct((PLANES * 16, lanes), bf16),
+            jax.ShapeDtypeStruct((8, 128), jnp.int32),
+        ],
+        scratch_shapes=[
+            pltpu.VMEM((2 * channels, tile_r, tile_c), bf16),
+            pltpu.VMEM((32, tile_r + 2 * TOP, STRIDE), f32),
+            pltpu.VMEM((2, 2 * channels, 16, tile_c), bf16),
+            pltpu.VMEM((2, 8, 2 * channels * tile_r), f32),
+            pltpu.VMEM((4, 2 * channels, 16, 128), bf16),
+            pltpu.VMEM((8, 2 * channels * tile_r), f32),
+            pltpu.VMEM((2, 8, 128), jnp.int32),
+            pltpu.SemaphoreType.DMA((2, 8)),
+            pltpu.SemaphoreType.DMA((2, 8)),
+        ],
+        compiler_params=pltpu.CompilerParams(
+            collective_id=2, has_side_effects=True, vmem_limit_bytes=VMEM
+        ),
+        name="frame",
+    )(*args)
 
 
 def run_pool(shape, per_slab, cells, *args):
@@ -610,101 +820,59 @@
     )(*args)
 
 
+def frame_constants(tile_c):
+    move = np.zeros((tile_c, STRIDE), np.float32)
+    move[np.arange(tile_c), HALO + np.arange(tile_c)] = 1
+    ends = np.zeros((8, tile_c), np.float32)
+    back = np.zeros((272, STRIDE), np.float32)
+    for x in range(HALO):
+        ends[x, x] = 1
+        ends[HALO + x, tile_c - HALO + x] = 1
+        back[128 - HALO + x, x] = 1
+        back[128 + x, HALO + tile_c + x] = 1
+        back[256 + HALO + x, x] = 1
+        back[264 + x, HALO + tile_c + x] = 1
+    return tuple(jnp.asarray(a, bf16) for a in (move, ends, back))
+
+
 def body(
     coarse, latent, noise_level, reg_first, reg_second, den_first, den_middle, den_pool, den_last,
     anchors, patch_count, patch_weight,
 ):
-    channels, tile_r, tile_c = latent.shape
-    inputs = coarse.shape[0]
+    tile_r, tile_c = latent.shape[1:]
     patch = patch_weight.shape[0]
-    rows = tile_r + 2 * HALO
+    rows = tile_r + 2 * TOP
     size = lanes_of(rows)
-    groups = rows // PLANES
-    used = groups * STRIDE
     slab = lax.axis_index("slab")
     column = lax.axis_index("patch")
-    scale_in, skip, scale_out = precondition(noise_level)
-
-    both = jnp.concatenate([coarse, (scale_in * latent).astype(bf16)], 0)
-    both = with_halo(with_halo(both, "slab", 1, HALO), "patch", 2, HALO)
-    both = jnp.pad(both, ((0, 0), (0, 0), (0, STRIDE - both.shape[2])))
-    both = both.reshape(inputs + channels, groups, PLANES, STRIDE).transpose(2, 0, 1, 3)
-    both = both.reshape(PLANES, inputs + channels, used)
-
-    def planes_of(part):
-        part = jnp.pad(part, ((0, 0), (0, 16 - part.shape[1]), (PAD, PAD + size - used)))
-        return part.reshape(PLANES * 16, size + 2 * PAD)
-
-    coarse_flat = planes_of(both[:, :inputs])
-    latent_flat = planes_of(both[:, inputs:])
-
-    table = jnp.concatenate([anchors[0], jnp.broadcast_to(patch_count[:, None], (1, 2))], 0)
-    tables = jnp.stack([passed(table, "slab", 1), table, passed(table, "slab", -1)], 0)
+    shape = (lax.axis_size("slab"), lax.axis_size("patch"))
     per_slab = anchors.shape[1]
-    live = jnp.arange(per_slab)[None, :] < tables[:, per_slab, :1]
-    tab_r = tables[:, :per_slab, 0] - slab * tile_r + HALO
-    tab_c = tables[:, :per_slab, 1] - column * tile_c + HALO
-    live = live & (tab_r < HALO + tile_r) & (tab_r + patch > HALO)
-    live = (live & (tab_c < HALO + tile_c) & (tab_c + patch > HALO)).reshape(-1)
-    far = 1 << 20
-    entries = 3 * per_slab
-    tab_r = jnp.where(live, tab_r.reshape(-1), far)
-    tab_c = jnp.where(live, tab_c.reshape(-1), far)
-    place = jnp.cumsum(live.astype(jnp.int32)) - 1
-    number = jnp.sum(live.astype(jnp.int32))
-    labels = jnp.arange(entries, dtype=jnp.int32)
-    hit = live[None, :] & (place[None, :] == labels[:, None])
-    order = jnp.sum(jnp.where(hit, labels[None, :], 0), 1)
-    top = HALO - slab * tile_r
+
+    labels = np.arange(per_slab, dtype=np.int32)
+    table = jnp.stack(
+        [anchors[0, :, 0], anchors[0, :, 1], jnp.broadcast_to(patch_count, (per_slab,)), labels], 0
+    )
+    table = jnp.pad(jnp.tile(table, (1, 3)), ((0, 4), (0, 128 - 3 * per_slab)))
+    coarse_flat, latent_flat, tabs = run_frame(
+        shape, per_slab, patch, latent.shape,
+        noise_level, coarse, latent, table, *frame_constants(tile_c),
+    )
+
+    top = TOP - slab * tile_r
     left = HALO - column * tile_c
-    meta = jnp.stack(
-        [
-            top, top + lax.axis_size("slab") * tile_r,
-            left, left + lax.axis_size("patch") * tile_c, number,
-        ]
-    ).astype(jnp.int32)
-
-    def gather_pair(weight):
-        taps = jnp.pad(jnp.transpose(weight, (1, 0, 2)), ((0, 0), (0, 0), (0, 16 - weight.shape[2])))
-        taps = taps.reshape(128, 144)
-        return jnp.concatenate(
-            [jnp.pad(taps, ((0, 0), (0, 48))), jnp.pad(taps, ((0, 0), (48, 0)))], 0
-        )
-
-    def spread_pair(weight, front):
-        taps = jnp.pad(weight, ((0, 0), (front, 16 - front - weight.shape[1]), (0, 0)))
-        taps = taps.reshape(3, 48, 128)[::-1].reshape(144, 128)
-        return jnp.concatenate(
-            [jnp.pad(taps, ((0, 48), (0, 0))), jnp.pad(taps, ((48, 0), (0, 0)))], 1
-        )
-
-    w1 = gather_pair(0.5 * reg_first)
-    w2 = spread_pair(reg_second, 4)
-    den = 0.5 * den_first
-    main = jnp.transpose(den[:, :, :16], (1, 0, 2)).reshape(128, 144)
-    rest = den[:, :, 16:]
-    side = [rest[t] for t in (0, 1, 3, 4, 6, 7, 2, 5, 8)] + [jnp.zeros_like(rest[0])]
-    w3 = jnp.concatenate([main] + side, 1)
-    wcol = jnp.pad(jnp.transpose(den, (0, 2, 1)), ((0, 0), (0, 32 - 2 * channels), (0, 0)))
-    wrow = jnp.stack([jnp.pad(wcol, ((0, 0), (32 * u, 96 - 32 * u), (0, 0))) for u in range(4)], 0)
-    w4 = (0.5 * den_middle).T
-    w5 = spread_pair(den_last, 0)
-
-    flat = jnp.arange(size, dtype=jnp.int32)
-    rowi = PLANES * (flat // STRIDE)[None] + jnp.arange(PLANES, dtype=jnp.int32)[:, None]
-    coli = jnp.broadcast_to(flat % STRIDE, (PLANES, size))
-    lanes_r = jnp.pad(tab_r, (0, 128 - entries), constant_values=far)[None]
-    lanes_c = jnp.pad(tab_c, (0, 128 - entries), constant_values=far)[None]
-
+    meta = jnp.stack([top, top + shape[0] * tile_r, left, left + shape[1] * tile_c])
+    flat = np.arange(size, dtype=np.int32)
+    rowi = PLANES * (flat // STRIDE)[None] + np.arange(PLANES, dtype=np.int32)[:, None]
+    coli = np.broadcast_to(flat % STRIDE, (PLANES, size))
     fixed = (rows, patch, tile_r, tile_c)
-    first, mean, part, ring, strips = run_regress(
-        fixed, entries,
-        meta, order, tab_r, tab_c,
-        coarse_flat, latent_flat, rowi, coli, lanes_r, lanes_c, w1, w2, w3, wrow, wcol,
+    first, mean, part, ring, strips, order = run_regress(
+        fixed, 3 * per_slab,
+        meta.astype(jnp.int32), tabs, coarse_flat, latent_flat,
+        jnp.asarray(rowi, jnp.int32), jnp.asarray(coli, jnp.int32),
+        tabs, reg_first, reg_second, den_first,
     )
 
-    shape = (lax.axis_size("slab"), lax.axis_size("patch"))
-    lift = run_pool(shape, per_slab, patch * patch, part, ring, den_pool.astype(f32))
+    lift = run_pool(shape, per_slab, patch * patch, part, ring, den_pool)
 
     weight = jnp.pad(patch_weight.astype(f32), ((0, 0), (0, STRIDE - patch)))
     weight = weight.reshape(patch // PLANES, PLANES, STRIDE).transpose(1, 0, 2)
@@ -712,20 +880,11 @@
     end = -weight.shape[1] % 128
     weight = jnp.pad(weight, ((0, 0), (WFRONT, end + WFRONT)))
     weight = weight.reshape(PLANES, -1, 128).transpose(1, 0, 2)
-    blended = run_patches(
-        fixed, meta, order, tab_r, tab_c, first, strips, lift, weight, w4, w5
+    next_state, estimate = run_patches(
+        fixed,
+        order, tabs, noise_level, first, strips, lift, weight, mean, latent, den_middle, den_last,
     )
-
-    def tile_of(flat):
-        planes = flat.reshape(PLANES, 16, size)[:, :, :used].reshape(PLANES, 16, groups, STRIDE)
-        whole = planes.transpose(1, 2, 0, 3).reshape(16, rows, STRIDE)
-        return whole[:, HALO : HALO + tile_r, HALO : HALO + tile_c]
-
-    blended = tile_of(blended)[:channels]
-    mean = tile_of(mean)[4:]
-    denoised = skip * latent + scale_out * blended
-    next_state = latent + (step_ratio - 1.0) * (latent - denoised)
-    return (next_state, mean + denoised)
+    return (next_state, estimate)
 
 
 def solution(mesh):

time: 216 us -> 158 us (0.73)
  the two profiles are of different devices: /device:TPU:22 before, /device:TPU:46 now
where the time goes in v3:
time: 158 us
  Pallas kernels  150 us (95%)
  local copies, waits for them, and re-layouts  5.09 us (3%)
  between operations  2.19 us (1%)
    pallas_call x1, Pallas kernels, run_patches(): pl.pallas_call(functools.partial(patch_kernel, *fixed), in_specs=[smem] *...  68.1 us
    pallas_call x1, Pallas kernels, run_regress(): pl.pallas_call(functools.partial(regress_kernel, *fixed), in_specs=[smem]...  52.5 us
    pallas_call x1, Pallas kernels, run_frame(): pl.pallas_call(functools.partial(frame_kernel, shape, per_slab, patch), i...  17.3 us
    pallas_call x1, Pallas kernels, run_pool(): pl.pallas_call(functools.partial(pool_kernel, shape, per_slab, cells), in...  12 us

profile of v3, /device:TPU:46, one launch (start us, length us, event | category | flops | bytes accessed | tf_op | source)
XLA Modules:
  0.0 157.9 jit_solution(13250902926963074682)
XLA Ops:
  0.6 0.0 copy-start.2
  0.6 0.6 pad_add_fusion.1.meta
  1.2 0.8 slice_bitcast_fusion.1
  2.6 0.1 pad.17.clone
  2.7 0.0 copy-start.1
  2.7 0.1 pad_add_fusion
  2.8 0.1 tile.10
  2.9 0.6 pad.12.table
  4.1 0.0 copy-start.3
  4.2 17.3 %frame.1 = (bf16[128,5632]{1,0:T(8,128)(2,1)}, bf16[128,5632]{1,0:T(8,128)(2,1)}, s32[8,128]{1,0:T(8,128)}) custom-call(f32[1]{0:T(128)S(6)} %copy.27.noise, bf16[12,128,256]{2,1,0:T(8,128)(2,1)} %coarse.1, f32[12,128,256]{2,1,0:T(8,128)} %latent.3, s32[8,128]{1,0:T(8,128)} %pad.12.table, bf16[256,264]{1,0:T(8,128)(2,1)} %constant.39.clone.move, ...), custom_call_target="tpu_custom_call" | custom-call | tf_op jit(solution)/shard_map/frame/pallas_call | solution.py:777
  21.4 0.0 copy-done.2
  21.4 0.9 copy.22.raw1
  22.3 0.0 copy-done.1
  22.3 0.9 copy.23.raw3
  23.2 0.0 copy-done.3
  23.2 0.7 jit_solution_.3.coli
  23.9 0.0 copy-start
  23.9 52.5 %regress.1 = (bf16[1024,4864]{1,0:T(8,128)(2,1)}, f32[128,4864]{1,0:T(8,128)}, f32[128,128]{1,0:T(8,128)}, f32[48,128]{1,0:T(8,128)}, bf16[48,928,128]{2,1,0:T(8,128)(2,1)}, /*index=5*/s32[49]{0:T(128)}) custom-call(s32[4]{0:T(128)} %pad_add_fusion.1.meta, s32[8,128]{1,0:T(8,128)} %get-tuple-element.11.tabs.tabs_v, ...), custom_call_target="tpu_custom_call" | custom-call | tf_op jit(solution)/shard_map/regress/pallas_call | solution.py:526
  76.4 12.0 %pool.2.lift = f32[48,128]{1,0:T(8,128)} custom-call(f32[128,128]{1,0:T(8,128)} %get-tuple-element.17.part, f32[48,128]{1,0:T(8,128)} %get-tuple-element.18.ring, bf16[128,128]{1,0:T(8,128)(2,1)} %pool.3), custom_call_target="tpu_custom_call" | custom-call | tf_op jit(solution)/shard_map/pool/pallas_call | solution.py:807
  88.5 0.0 copy-done
  88.6 0.1 copy.26
  88.6 0.2 reshape.21
  88.8 0.8 pad_bitcast_fusion.weight
  89.6 68.1 %patches.1 = (f32[12,128,256]{2,1,0:T(8,128)}, f32[12,128,256]{2,1,0:T(8,128)}) custom-call(s32[49]{0:T(128)} %get-tuple-element.14.order, s32[8,128]{1,0:T(8,128)} %get-tuple-element.11.tabs.tabs_v, f32[1]{0:T(128)S(6)} %copy.27.noise, bf16[1024,4864]{1,0:T(8,128)(2,1)} %get-tuple-element.15.first, bf16[48,928,128]{2,1,0:T(8,128)(2,1)} %get-tuple-element.16.strips, ...), custom_call_target="tpu_custom_call" | custom-call | tf_op jit(solution)/shard_map/patches/pallas_call | solution.py:558
  (4 shorter events, 0.1 us)
Async XLA Ops:
  0.6 20.8 %copy-start.2 = (bf16[9,128,12]{1,2,0:T(8,128)(2,1)S(1)}, bf16[9,128,12]{1,2,0:T(8,128)(2,1)}, u32[]{:S(2)}) copy-start(bf16[9,128,12]{1,2,0:T(8,128)(2,1)} %param.21) | copy-start | bytes 82948
  2.7 19.6 %copy-start.1 = (bf16[9,128,24]{1,2,0:T(8,128)(2,1)S(1)}, bf16[9,128,24]{1,2,0:T(8,128)(2,1)}, u32[]{:S(2)}) copy-start(bf16[9,128,24]{1,2,0:T(8,128)(2,1)} %param.23) | copy-start | bytes 165892
  4.1 19.1 %copy-start.3 = (s32[4864]{0:T(1024)S(1)}, s32[4864]{0:T(1024)}, u32[]{:S(2)}) copy-start(s32[4864]{0:T(1024)} %constant.43.clone) | copy-start | bytes 58372
  23.9 64.6 %copy-start = (s32[224,224]{1,0:T(8,128)S(1)}, s32[224,224]{1,0:T(8,128)}, u32[]{:S(2)}) copy-start(s32[224,224]{1,0:T(8,128)} %param.29) | copy-start | bytes 602116

commit v4 on v3

--- a/solution.py
+++ b/solution.py
@@ -18,6 +18,7 @@
 PLANES = 8
 PAD = 384
 FRONT = 528
+LAG = 3
 STEP = 256
 TILE = 512
 COLUMN = 24
@@ -78,14 +79,20 @@
     return planes
 
 
-def gather_pair(raw, out):
-    zero = jnp.zeros((128, 16 - raw.shape[2]), bf16)
+def taps_of(raw, lo, hi, count):
     parts = []
     for t in range(9):
-        parts += [raw[t] * 0.5, zero]
-    gap = jnp.zeros((128, 48), bf16)
-    out[:128, :] = jnp.concatenate(parts + [gap], 1)
-    out[128:, :] = jnp.concatenate([gap] + parts, 1)
+        parts.append(0.5 * raw[t].astype(f32)[lo:hi])
+        if hi - lo < count:
+            parts.append(jnp.zeros((count - hi + lo, 128), f32))
+    return parts
+
+
+def gather_pair(raw, out):
+    gap = [jnp.zeros((48, 128), f32)]
+    parts = taps_of(raw, 0, raw.shape[1], 16)
+    out[:128, :] = jnp.concatenate(parts + gap, 0).T.astype(bf16)
+    out[128:, :] = jnp.concatenate(gap + parts, 0).T.astype(bf16)
 
 
 def spread_pair(raw, out, front):
@@ -102,7 +109,7 @@
 
 def regress_kernel(
     rows, patch, tile_r, tile_c,
-    meta, tabs, coarse, latent, rowi, coli, tabs_v, raw1, raw2, raw3,
+    meta, tabs, coarse, latent, tabs_v, raw1, raw2, raw3,
     first_out, mean_out, part_out, ring_out, strips_out, order,
     w1, w2, w3, sums, cond_a, cond_b, cond_c, sbuf, sem,
 ):
@@ -113,11 +120,9 @@
     row_lo, row_hi, col_lo, col_hi = meta[0], meta[1], meta[2], meta[3]
     gather_pair(raw1, w1)
     spread_pair(raw2, w2, 4)
-    zero8 = jnp.zeros((128, 8), bf16)
-    w3[...] = 0.5 * jnp.concatenate(
-        [raw3[t][:, :16] for t in range(9)]
-        + [raw3[t][:, 16:] for t in (0, 1, 3, 4, 6, 7, 2, 5, 8)] + [zero8], 1
-    )
+    side = taps_of(raw3, 16, 24, 8)
+    side = [side[t] for t in (0, 1, 3, 4, 6, 7, 2, 5, 8)] + [jnp.zeros((8, 128), f32)]
+    w3[...] = jnp.concatenate(taps_of(raw3, 0, 16, 16) + side, 0).T.astype(bf16)
 
     def enlist(q, n):
         live = tabs[0, q] < FAR
@@ -139,12 +144,14 @@
     cond_c[cells : cells + FRONT, :] = jnp.zeros((FRONT, 128), f32)
     cond_c[cells + FRONT + size :, :] = jnp.zeros((cond_c.shape[0] - cells - FRONT - size, 128), f32)
 
-    @pl.loop(0, steps, unroll=4)
-    def _(k):
+    def stage1(k):
         base = pl.multiple_of(k * STEP, 128)
         x = shifted(coarse, base, STEP, 16)
-        row = rowi[:, pl.ds(base, STEP)]
-        col = coli[:, pl.ds(base, STEP)]
+        group = base // STRIDE
+        lane = lax.broadcasted_iota(jnp.int32, (PLANES, STEP), 1)
+        later = (lane >= (group + 1) * STRIDE - base).astype(jnp.int32)
+        col = lane + base - (group + later) * STRIDE
+        row = (group + later) * PLANES + lax.broadcasted_iota(jnp.int32, (PLANES, STEP), 0)
         inside = (row >= row_lo) & (row < row_hi) & (col >= col_lo) & (col < col_hi)
         keep = jnp.where(inside, 1.0, 0.0)
         parts = []
@@ -163,8 +170,7 @@
             parts.append(jnp.dot(w2[...], h, preferred_element_type=f32))
         sums[:, pl.ds(base + PAD, STEP)] = jnp.concatenate(overlapped(parts), 0)
 
-    @pl.loop(0, steps, unroll=4)
-    def _(k):
+    def stage2(k):
         base = pl.multiple_of(k * STEP, 128)
         means = combined(sums, base, STEP)
         lat = latent[:, pl.ds(base + PAD, STEP)].astype(f32)
@@ -186,10 +192,7 @@
                     :, 128 * j : 128 * j + 128
                 ].T
 
-    part_out[...] = jnp.zeros_like(part_out)
-
-    @pl.loop(0, steps, unroll=4)
-    def _(k):
+    def stage3(k):
         base = pl.multiple_of(k * STEP, 128)
         xa = shifted(cond_a, base, STEP, 16)
         xb = shifted(cond_b, base, STEP, 8)
@@ -234,17 +237,52 @@
             jnp.concatenate(firsts, 1), jnp.concatenate(masks, 0), preferred_element_type=f32
         )
 
+    part_out[...] = jnp.zeros_like(part_out)
+
+    @pl.loop(0, LAG, unroll=LAG)
+    def _(k):
+        stage1(k)
+
+    @pl.loop(LAG, 2 * LAG, unroll=LAG)
+    def _(k):
+        stage2(k - LAG)
+        stage1(k)
+
+    @pl.loop(2 * LAG, steps)
+    def _(k):
+        stage3(k - 2 * LAG)
+        stage2(k - LAG)
+        stage1(k)
+
+    @pl.loop(steps - LAG, steps, unroll=LAG)
+    def _(k):
+        stage3(k - LAG)
+        stage2(k)
+
+    @pl.loop(steps - LAG, steps, unroll=LAG)
+    def _(k):
+        stage3(k)
+
     ring_out[...] = jnp.zeros_like(ring_out)
     j = lax.broadcasted_iota(jnp.int32, (STRIDE, 128), 0)
     g = lax.broadcasted_iota(jnp.int32, (COLUMN, 128), 0)
     i = jnp.concatenate([g * PLANES + p for p in range(PLANES)], 0)
     live = jnp.concatenate([g < groups for p in range(PLANES)], 0)
 
+    def put(n):
+        return pltpu.make_async_copy(sbuf.at[n % 2], strips_out.at[n], sem.at[n % 2])
+
     @pl.loop(0, number)
     def _(n):
         q = order[n]
         r0, c0 = tabs[0, q], tabs[1, q]
         r1, c1 = r0 + patch - 1, c0 + patch - 1
+
+        slot = n % 2
+
+        @pl.when(n >= 2)
+        def _():
+            put(n - 2).wait()
 
         def add(value, weight):
             got = jnp.sum(jnp.where(weight, value.astype(f32), 0.0), 0, keepdims=True)
@@ -263,13 +301,13 @@
                         x = cond_c[pl.ds(start + b - 1, STRIDE), :]
                         x = jnp.where((j + (b - 1) >= c0) & (j + (b - 1) <= c1), x, 0.0)
                         x = pltpu.roll(x, (128 - plane % 4 * 32) % 128, 1)[:, :24].astype(bf16)
-                        term = lax.dot_general(
-                            x, raw3[3 * a + b], (((1,), (1,)), ((), ())), preferred_element_type=f32
-                        )
+                        term = jnp.dot(x, raw3[3 * a + b], preferred_element_type=f32)
                         total = term if total is None else total + term
                 value = silu_half(0.5 * total)
                 tail = jnp.zeros((STRIP - STRIDE, 128), f32)
-                sbuf[STRIP * s : STRIP * s + STRIP, :] = jnp.concatenate([value, tail], 0).astype(bf16)
+                sbuf[slot, STRIP * s : STRIP * s + STRIP, :] = jnp.concatenate(
+                    [value, tail], 0
+                ).astype(bf16)
                 value = value.astype(bf16)
                 own = (r >= TOP) & (r < TOP + tile_r)
                 add(value, own & (j >= c0) & (j <= c1) & (j >= HALO) & (j < HALO + tile_c))
@@ -295,19 +333,21 @@
                         x = jnp.concatenate(planes[a : a + PLANES], 0)
                         inside = (i + (a - 1) >= r0) & (i + (a - 1) <= r1)
                         x = jnp.where(inside[:, :32], x, 0.0)[:, :24].astype(bf16)
-                        term = lax.dot_general(
-                            x, raw3[3 * a + b], (((1,), (1,)), ((), ())), preferred_element_type=f32
-                        )
+                        term = jnp.dot(x, raw3[3 * a + b], preferred_element_type=f32)
                         total = term if total is None else total + term
                 value = silu_half(0.5 * total).astype(bf16)
                 lo = 2 * STRIP + PLANES * COLUMN * s
-                sbuf[lo : lo + PLANES * COLUMN, :] = value
+                sbuf[slot, lo : lo + PLANES * COLUMN, :] = value
                 own = (c >= HALO) & (c < HALO + tile_c) & live
                 add(value, own & (i > r0) & (i < r1) & (i >= TOP) & (i < TOP + tile_r))
 
-        copy = pltpu.make_async_copy(sbuf, strips_out.at[n], sem)
-        copy.start()
-        copy.wait()
+        put(n).start()
+
+    for back in (2, 1):
+
+        @pl.when(number >= back)
+        def _(back=back):
+            put(number - back).wait()
 
 
 def patch_kernel(
@@ -525,7 +565,7 @@
     cells = size + 2 * FRONT
     return pl.pallas_call(
         functools.partial(regress_kernel, *fixed),
-        in_specs=[smem] * 2 + [vmem] * 8,
+        in_specs=[smem] * 2 + [vmem] * 6,
         out_specs=[vmem, vmem, vmem, vmem, anyw, smem],
         out_shape=[
             jax.ShapeDtypeStruct((PLANES * 128, size), bf16),
@@ -543,8 +583,8 @@
             pltpu.VMEM((16 * PLANES, size + 2 * PAD), bf16),
             pltpu.VMEM((8 * PLANES, size + 2 * PAD), f32),
             pltpu.VMEM((2 * cells + COLUMN * STRIDE - size + STRIDE, 128), f32),
-            pltpu.VMEM((2 * (STRIP + PLANES * COLUMN), 128), bf16),
-            pltpu.SemaphoreType.DMA,
+            pltpu.VMEM((2, 2 * (STRIP + PLANES * COLUMN), 128), bf16),
+            pltpu.SemaphoreType.DMA((2,)),
         ],
         compiler_params=pltpu.CompilerParams(vmem_limit_bytes=VMEM),
         name="regress",
@@ -842,7 +882,6 @@
     tile_r, tile_c = latent.shape[1:]
     patch = patch_weight.shape[0]
     rows = tile_r + 2 * TOP
-    size = lanes_of(rows)
     slab = lax.axis_index("slab")
     column = lax.axis_index("patch")
     shape = (lax.axis_size("slab"), lax.axis_size("patch"))
@@ -861,15 +900,11 @@
     top = TOP - slab * tile_r
     left = HALO - column * tile_c
     meta = jnp.stack([top, top + shape[0] * tile_r, left, left + shape[1] * tile_c])
-    flat = np.arange(size, dtype=np.int32)
-    rowi = PLANES * (flat // STRIDE)[None] + np.arange(PLANES, dtype=np.int32)[:, None]
-    coli = np.broadcast_to(flat % STRIDE, (PLANES, size))
     fixed = (rows, patch, tile_r, tile_c)
     first, mean, part, ring, strips, order = run_regress(
         fixed, 3 * per_slab,
-        meta.astype(jnp.int32), tabs, coarse_flat, latent_flat,
-        jnp.asarray(rowi, jnp.int32), jnp.asarray(coli, jnp.int32),
-        tabs, reg_first, reg_second, den_first,
+        meta.astype(jnp.int32), tabs, coarse_flat, latent_flat, tabs,
+        jnp.transpose(reg_first, (0, 2, 1)), reg_second, jnp.transpose(den_first, (0, 2, 1)),
     )
 
     lift = run_pool(shape, per_slab, patch * patch, part, ring, den_pool)

time: 158 us -> 156 us (0.987)
  the two profiles are of different devices: /device:TPU:46 before, /device:TPU:124 now
where the time goes in v4:
time: 156 us; the launch traced here: 155 us
  Pallas kernels  149 us (96%)
  local copies, waits for them, and re-layouts  2.59 us (2%)
  between operations  2.16 us (1%)
  other arithmetic  1.59 us (1%)
    pallas_call x1, Pallas kernels, run_patches(): pl.pallas_call(functools.partial(patch_kernel, *fixed), in_specs=[smem] *...  75.1 us
    pallas_call x1, Pallas kernels, run_regress(): pl.pallas_call(functools.partial(regress_kernel, *fixed), in_specs=[smem]...  48 us
    pallas_call x1, Pallas kernels, run_frame(): pl.pallas_call(functools.partial(frame_kernel, shape, per_slab, patch), i...  17.7 us
    pallas_call x1, Pallas kernels, run_pool(): pl.pallas_call(functools.partial(pool_kernel, shape, per_slab, cells), in...  8.33 us

profile of v4, /device:TPU:124, one launch (start us, length us, event | category | flops | bytes accessed | tf_op | source)
XLA Modules:
  0.0 155.4 jit_solution(8121163493616104305)
XLA Ops:
  1.9 0.6 pad_add_fusion.1.meta
  2.5 0.1 pad.17.clone
  2.6 0.8 slice_bitcast_fusion.1
  3.3 0.1 pad_add_fusion
  3.4 0.1 tile.10
  3.5 0.6 pad.12.table
  4.1 1.0 convert_element_type.7
  5.1 0.1 copy.20
  5.2 0.2 reshape.21
  5.4 0.8 pad_bitcast_fusion.weight
  6.1 17.7 %frame.1 = (bf16[128,5632]{1,0:T(8,128)(2,1)}, bf16[128,5632]{1,0:T(8,128)(2,1)}, s32[8,128]{1,0:T(8,128)}) custom-call(f32[1]{0:T(128)S(6)} %copy.21.noise, bf16[12,128,256]{2,1,0:T(8,128)(2,1)} %coarse.1, f32[12,128,256]{2,1,0:T(8,128)} %latent.3, s32[8,128]{1,0:T(8,128)} %pad.12.table, bf16[256,264]{1,0:T(8,128)(2,1)} %constant.35.clone.move, ...), custom_call_target="tpu_custom_call" | custom-call | tf_op jit(solution)/shard_map/frame/pallas_call | solution.py:817
  23.8 48.0 %regress.1 = (bf16[1024,4864]{1,0:T(8,128)(2,1)}, f32[128,4864]{1,0:T(8,128)}, f32[128,128]{1,0:T(8,128)}, f32[48,128]{1,0:T(8,128)}, bf16[48,928,128]{2,1,0:T(8,128)(2,1)}, /*index=5*/s32[49]{0:T(128)}) custom-call(s32[4]{0:T(128)} %pad_add_fusion.1.meta, s32[8,128]{1,0:T(8,128)} %get-tuple-element.11.tabs.tabs_v, ...), custom_call_target="tpu_custom_call" | custom-call | tf_op jit(solution)/shard_map/regress/pallas_call | solution.py:566
  71.8 8.3 %pool.2.lift = f32[48,128]{1,0:T(8,128)} custom-call(f32[128,128]{1,0:T(8,128)} %get-tuple-element.17.part, f32[48,128]{1,0:T(8,128)} %get-tuple-element.18.ring, bf16[128,128]{1,0:T(8,128)(2,1)} %pool.3), custom_call_target="tpu_custom_call" | custom-call | tf_op jit(solution)/shard_map/pool/pallas_call | solution.py:847
  80.1 75.1 %patches.1 = (f32[12,128,256]{2,1,0:T(8,128)}, f32[12,128,256]{2,1,0:T(8,128)}) custom-call(s32[49]{0:T(128)} %get-tuple-element.14.order, s32[8,128]{1,0:T(8,128)} %get-tuple-element.11.tabs.tabs_v, f32[1]{0:T(128)S(6)} %copy.21.noise, bf16[1024,4864]{1,0:T(8,128)(2,1)} %get-tuple-element.15.first, bf16[48,928,128]{2,1,0:T(8,128)(2,1)} %get-tuple-element.16.strips, ...), custom_call_target="tpu_custom_call" | custom-call | tf_op jit(solution)/shard_map/patches/pallas_call | solution.py:598
  (3 shorter events, 0.0 us)

commit v5 on v4

--- a/solution.py
+++ b/solution.py
@@ -111,7 +111,7 @@
     rows, patch, tile_r, tile_c,
     meta, tabs, coarse, latent, tabs_v, raw1, raw2, raw3,
     first_out, mean_out, part_out, ring_out, strips_out, order,
-    w1, w2, w3, sums, cond_a, cond_b, cond_c, sbuf, sem,
+    w1, w2, w3, sums, cond_a, cond_b, cond_c, fbuf, sbuf, sem, fsem,
 ):
     size = lanes_of(rows)
     steps = size // STEP
@@ -192,7 +192,12 @@
                     :, 128 * j : 128 * j + 128
                 ].T
 
+    def put_first(k):
+        at = pl.ds(pl.multiple_of(k * STEP, 128), STEP)
+        return pltpu.make_async_copy(fbuf.at[k % 2], first_out.at[:, at], fsem.at[k % 2])
+
     def stage3(k):
+        slot = k % 2
         base = pl.multiple_of(k * STEP, 128)
         xa = shifted(cond_a, base, STEP, 16)
         xb = shifted(cond_b, base, STEP, 8)
@@ -229,7 +234,7 @@
                 0,
             )
             first = silu_half(jnp.dot(w3[...], stack, preferred_element_type=f32)).astype(bf16)
-            first_out[128 * i : 128 * i + 128, pl.ds(base, STEP)] = first
+            fbuf[slot, 128 * i : 128 * i + 128, :] = first
             firsts.append(first)
             row = group * PLANES + i
             masks.append(now * row_keep(row) + late * row_keep(row + PLANES))
@@ -248,20 +253,32 @@
         stage2(k - LAG)
         stage1(k)
 
-    @pl.loop(2 * LAG, steps)
+    for k in range(2):
+        stage3(k)
+        stage2(k + LAG)
+        stage1(k + 2 * LAG)
+        put_first(k).start()
+
+    @pl.loop(2 * LAG + 2, steps)
     def _(k):
+        put_first(k - 2 * LAG - 2).wait()
         stage3(k - 2 * LAG)
         stage2(k - LAG)
         stage1(k)
-
-    @pl.loop(steps - LAG, steps, unroll=LAG)
+        put_first(k - 2 * LAG).start()
+
+    @pl.loop(steps - LAG, steps)
     def _(k):
+        put_first(k - LAG - 2).wait()
         stage3(k - LAG)
         stage2(k)
-
-    @pl.loop(steps - LAG, steps, unroll=LAG)
+        put_first(k - LAG).start()
+
+    @pl.loop(steps - LAG, steps)
     def _(k):
+        put_first(k - 2).wait()
         stage3(k)
+        put_first(k).start()
 
     ring_out[...] = jnp.zeros_like(ring_out)
     j = lax.broadcasted_iota(jnp.int32, (STRIDE, 128), 0)
@@ -343,6 +360,8 @@
 
         put(n).start()
 
+    put_first(steps - 2).wait()
+    put_first(steps - 1).wait()
     for back in (2, 1):
 
         @pl.when(number >= back)
@@ -566,7 +585,7 @@
     return pl.pallas_call(
         functools.partial(regress_kernel, *fixed),
         in_specs=[smem] * 2 + [vmem] * 6,
-        out_specs=[vmem, vmem, vmem, vmem, anyw, smem],
+        out_specs=[anyw, vmem, vmem, vmem, anyw, smem],
         out_shape=[
             jax.ShapeDtypeStruct((PLANES * 128, size), bf16),
             jax.ShapeDtypeStruct((PLANES * 16, size), f32),
@@ -583,7 +602,9 @@
             pltpu.VMEM((16 * PLANES, size + 2 * PAD), bf16),
             pltpu.VMEM((8 * PLANES, size + 2 * PAD), f32),
             pltpu.VMEM((2 * cells + COLUMN * STRIDE - size + STRIDE, 128), f32),
+            pltpu.VMEM((2, PLANES * 128, STEP), bf16),
             pltpu.VMEM((2, 2 * (STRIP + PLANES * COLUMN), 128), bf16),
+            pltpu.SemaphoreType.DMA((2,)),
             pltpu.SemaphoreType.DMA((2,)),
         ],
         compiler_params=pltpu.CompilerParams(vmem_limit_bytes=VMEM),

time: 156 us -> 133 us (0.85)
  the two profiles are of different devices: /device:TPU:124 before, /device:TPU:38 now
where the time goes in v5:
time: 133 us; the launch traced here: 132 us
  Pallas kernels  126 us (95%)
  local copies, waits for them, and re-layouts  2.59 us (2%)
  between operations  2.16 us (2%)
  other arithmetic  1.59 us (1%)
    pallas_call x1, Pallas kernels, run_patches(): pl.pallas_call(functools.partial(patch_kernel, *fixed), in_specs=[smem] *...  57.1 us
    pallas_call x1, Pallas kernels, run_regress(): pl.pallas_call(functools.partial(regress_kernel, *fixed), in_specs=[smem]...  40.4 us
    pallas_call x1, Pallas kernels, run_frame(): pl.pallas_call(functools.partial(frame_kernel, shape, per_slab, patch), i...  18.3 us
    pallas_call x1, Pallas kernels, run_pool(): pl.pallas_call(functools.partial(pool_kernel, shape, per_slab, cells), in...  10.3 us

profile of v5, /device:TPU:38, one launch (start us, length us, event | category | flops | bytes accessed | tf_op | source)
XLA Modules:
  0.0 132.5 jit_solution(8356658246685001904)
XLA Ops:
  1.9 0.6 pad_add_fusion.1.meta
  2.5 0.1 pad.17.clone
  2.6 0.8 slice_bitcast_fusion.1
  3.3 0.1 pad_add_fusion
  3.4 0.1 tile.10
  3.5 0.6 pad.12.table
  4.1 1.0 convert_element_type.7
  5.1 0.1 copy.20
  5.2 0.2 reshape.21
  5.4 0.8 pad_bitcast_fusion.weight
  6.1 18.3 %frame.1 = (bf16[128,5632]{1,0:T(8,128)(2,1)}, bf16[128,5632]{1,0:T(8,128)(2,1)}, s32[8,128]{1,0:T(8,128)}) custom-call(f32[1]{0:T(128)S(6)} %copy.21.noise, bf16[12,128,256]{2,1,0:T(8,128)(2,1)} %coarse.1, f32[12,128,256]{2,1,0:T(8,128)} %latent.3, s32[8,128]{1,0:T(8,128)} %pad.12.table, bf16[256,264]{1,0:T(8,128)(2,1)} %constant.35.clone.move, ...), custom_call_target="tpu_custom_call" | custom-call | tf_op jit(solution)/shard_map/frame/pallas_call | solution.py:838
  24.4 40.4 %regress.1 = (bf16[1024,4864]{1,0:T(8,128)(2,1)}, f32[128,4864]{1,0:T(8,128)}, f32[128,128]{1,0:T(8,128)}, f32[48,128]{1,0:T(8,128)}, bf16[48,928,128]{2,1,0:T(8,128)(2,1)}, /*index=5*/s32[49]{0:T(128)}) custom-call(s32[4]{0:T(128)} %pad_add_fusion.1.meta, s32[8,128]{1,0:T(8,128)} %get-tuple-element.11.tabs.tabs_v, ...), custom_call_target="tpu_custom_call" | custom-call | tf_op jit(solution)/shard_map/regress/pallas_call | solution.py:585
  64.9 10.3 %pool.2.lift = f32[48,128]{1,0:T(8,128)} custom-call(f32[128,128]{1,0:T(8,128)} %get-tuple-element.17.part, f32[48,128]{1,0:T(8,128)} %get-tuple-element.18.ring, bf16[128,128]{1,0:T(8,128)(2,1)} %pool.3), custom_call_target="tpu_custom_call" | custom-call | tf_op jit(solution)/shard_map/pool/pallas_call | solution.py:868
  75.2 57.1 %patches.1 = (f32[12,128,256]{2,1,0:T(8,128)}, f32[12,128,256]{2,1,0:T(8,128)}) custom-call(s32[49]{0:T(128)} %get-tuple-element.14.order, s32[8,128]{1,0:T(8,128)} %get-tuple-element.11.tabs.tabs_v, f32[1]{0:T(128)S(6)} %copy.21.noise, bf16[1024,4864]{1,0:T(8,128)(2,1)} %get-tuple-element.15.first, bf16[48,928,128]{2,1,0:T(8,128)(2,1)} %get-tuple-element.16.strips, ...), custom_call_target="tpu_custom_call" | custom-call | tf_op jit(solution)/shard_map/patches/pallas_call | solution.py:619
  (3 shorter events, 0.0 us)
